TPU v7x, 256 devices: a whole 4x4x8 slice. The times are simulated.
256 devices in a mesh: vol: 16 (over y, z_hi, core), ctl: 16 (over x, z_lo).
Axes of the slice: x: 4, y: 4, z: 8 (z_hi: 2, z_lo: 4; z = z_hi * 4 + z_lo), core: 2. Of those that a mesh axis runs over, the one named last changes fastest.
Arguments:
- vol_coords: bfloat16 [3, 65536], P(None, ('vol', 'ctl')), may hold values from 0 to 1
- vol_cotangent: bfloat16 [48, 65536], P(None, ('vol', 'ctl')), may hold values from -0.59765625 to 0.59765625
- ctl_coords: bfloat16 [3, 65536], P(None, ('ctl', 'vol')), may hold values from 0 to 1
- ctl_weights: bfloat16 [48, 65536], P(None, ('ctl', 'vol')), may hold values from -0.029907227 to 0.029907227
Outputs:
- weight_grad: float32 [48, 65536], P(None, ('ctl', 'vol'))
- vol_coord_grad: float32 [3, 65536], P(None, ('vol', 'ctl'))
- ctl_coord_grad: float32 [3, 65536], P(None, ('ctl', 'vol'))
All inputs are finite; a program needn't handle non-finite values.
Results may differ from a plain program's by a relative error of at most 0.0028.
Values may be sent and summed in bfloat16 or wider, within the bound.
No kernel may reach another device: no remote copies, remote signals or barrier semaphores. Data moves between devices by JAX's collectives and lax.ppermute only.
A program may use at most 64 MiB of HBM per device.

v0:
```python
import functools

import jax
import jax.numpy as jnp
from jax import lax
from jax.experimental import pallas as pl
from jax.experimental.pallas import tpu as pltpu
from jax.sharding import PartitionSpec as P

F32 = jnp.float32
BF = jnp.bfloat16
VMEM = pltpu.VMEM
WIDE = 64
BLOCK = 256
SLOPE = -320.0


def split3(total):
    first = total.astype(BF)
    rest = total - first.astype(F32)
    second = rest.astype(BF)
    third = (rest - second.astype(F32)).astype(BF)
    return (first, second, third)


def pack_kernel(vx_ref, vc_ref, cx_ref, cw_ref, v_ref, c_ref):
    ones = jnp.ones((3, BLOCK), BF)
    blank = jnp.zeros((7, BLOCK), BF)
    v = vx_ref[...].astype(F32) * 4.0
    v_len = jnp.concatenate(split3(jnp.sum(v * v, axis=0, keepdims=True)), axis=0)
    v_ref[0, 0:48, :] = vc_ref[...]
    v_ref[0, 48:64, :] = jnp.concatenate([(v * -2.0).astype(BF), v_len, ones, blank], axis=0)
    c = cx_ref[...].astype(F32) * 4.0
    c_len = jnp.concatenate(split3(jnp.sum(c * c, axis=0, keepdims=True)), axis=0)
    c_ref[0, 0:48, :] = cw_ref[...]
    c_ref[0, 48:64, :] = jnp.concatenate([c.astype(BF), ones, c_len, blank], axis=0)


def pack(vol_coords, vol_cotangent, ctl_coords, ctl_weights):
    packed = jax.ShapeDtypeStruct((1, WIDE, BLOCK), BF)
    return pl.pallas_call(
        pack_kernel,
        out_shape=(packed, packed),
        in_specs=[pl.BlockSpec(memory_space=VMEM)] * 4,
        out_specs=[pl.BlockSpec(memory_space=VMEM)] * 2,
    )(vol_coords, vol_cotangent, ctl_coords, ctl_weights)


def pair_kernel(unroll, v_lows, c_lows, c_begins, v_begin, *refs):
    refs = list(refs)
    v_parts = [refs.pop(0) for _ in v_lows]
    c_parts = [refs.pop(0) for _ in c_lows]
    c_starts = [refs.pop(0) for _ in c_begins]
    v_starts = [refs.pop(0) if begin else None for begin in v_begin]
    c_out = refs.pop(0)
    v_outs = [refs.pop(0) for _ in v_lows]
    v_all, v_tall, c_two, c_pos, v_sum = refs
    at = 0
    for part, low in zip(v_parts, v_lows):
        for slot in range(4):
            block = part[low + slot]
            v_all[:, at : at + BLOCK] = block
            v_tall[at : at + BLOCK, :] = block.T
            at += BLOCK
    rows = lax.broadcasted_iota(jnp.int32, (WIDE, BLOCK), 0)
    count = 0
    for part, low in zip(c_parts, c_lows):
        for slot in range(4):
            block = part[low + slot]
            blank = jnp.zeros_like(block)
            c_two[count, :, :BLOCK] = jnp.where(rows >= 48, block, blank)
            c_two[count, :, BLOCK:] = jnp.where(rows < 48, block, blank)
            c_pos[count] = block[48:64]
            count += 1
    v_sum[...] = jnp.zeros_like(v_sum)

    def tile(n, carry):
        both = jnp.dot(v_tall[...], c_two[n], preferred_element_type=F32)
        squared = jnp.maximum(both[:, :BLOCK], 1e-20)
        pair_dot = both[:, BLOCK:]
        inside = jnp.maximum(1.0 - squared * lax.rsqrt(squared), 0.0)
        second = inside * inside
        kernel = (second * second * (inside - 1.25)).astype(BF)
        weighting = (second * inside * pair_dot).astype(BF)
        weight_grad = jnp.dot(v_all[0:48, :], kernel, preferred_element_type=F32)
        pushed = jnp.dot(v_all[48:64, :], weighting, preferred_element_type=F32)
        own = c_pos[n]
        v_sum[...] += lax.dot_general(
            own, weighting, (((1,), (1,)), ((), ())), preferred_element_type=F32
        )
        ctl_pos = own[0:3].astype(F32) * 0.25
        grad = (ctl_pos * pushed[6:7] + pushed[0:3] * 0.125) * SLOPE
        found = jnp.concatenate([weight_grad * -4.0, grad, jnp.zeros((5, BLOCK), F32)], axis=0)
        for start, begin in zip(c_starts, c_begins):
            found = found + start[begin + n]
        c_out[n] = found
        return carry

    lax.fori_loop(0, count, tile, 0, unroll=unroll)
    at = 0
    for part, start in zip(v_outs, v_starts):
        for slot in range(4):
            pulled = v_sum[:, at : at + BLOCK]
            vol_pos = v_all[48:64, at : at + BLOCK][0:3].astype(F32) * -0.125
            grad = (vol_pos * pulled[3:4] - pulled[0:3] * 0.25) * SLOPE
            found = jnp.concatenate([grad, jnp.zeros((5, BLOCK), F32)], axis=0)
            part[slot] = found if start is None else found + start[slot]
            at += BLOCK


def pair_sums(v_parts, c_parts, v_starts, c_starts=()):
    v_count = 4 * len(v_parts)
    c_count = 4 * len(c_parts)
    extra = [start for start, _ in c_starts] + [start for start in v_starts if start is not None]
    args = [part for part, _ in [*v_parts, *c_parts]] + extra
    body = functools.partial(
        pair_kernel,
        max(1, UNROLL // v_count),
        [low for _, low in v_parts],
        [low for _, low in c_parts],
        [begin for _, begin in c_starts],
        [start is not None for start in v_starts],
    )
    outs = pl.pallas_call(
        body,
        out_shape=[jax.ShapeDtypeStruct((c_count, 56, BLOCK), F32)]
        + [jax.ShapeDtypeStruct((4, 8, BLOCK), F32)] * len(v_parts),
        in_specs=[pl.BlockSpec(memory_space=VMEM)] * len(args),
        out_specs=[pl.BlockSpec(memory_space=VMEM)] * (1 + len(v_parts)),
        scratch_shapes=[
            VMEM((WIDE, v_count * BLOCK), BF),
            VMEM((v_count * BLOCK, WIDE), BF),
            VMEM((c_count, WIDE, 2 * BLOCK), BF),
            VMEM((c_count, 16, BLOCK), BF),
            VMEM((16, v_count * BLOCK), F32),
        ],
        compiler_params=pltpu.CompilerParams(vmem_limit_bytes=48 * 2**20),
        cost_estimate=pl.CostEstimate(
            flops=v_count * c_count * 2 * 10**8, bytes_accessed=4 * 10**6, transcendentals=0
        ),
    )(*args)
    return outs


def swap(value, mask):
    return lax.ppermute(value, ("vol", "ctl"), [(i, i ^ mask) for i in range(256)])


def gather(value, masks):
    return jnp.concatenate([value] + [swap(value, mask) for mask in masks], axis=0)


def back(value, masks):
    return [swap(value[s + 1], mask) for s, mask in enumerate(masks)]


def tie(*values):
    return lax.optimization_barrier(values)


UNROLL = 8
X_MASKS = (4, 12, 8)
Y_MASKS = (64, 192, 128)
CORE, Z_ONE, Z_TWO, Z_SIX = (16, 1, 2, 34)


def shards(vol_coords, vol_cotangent, ctl_coords, ctl_weights):
    v, c = pack(vol_coords, vol_cotangent, ctl_coords, ctl_weights)
    cp, va = tie(gather(c, Y_MASKS), gather(v, X_MASKS))
    cq = swap(cp, CORE)
    cr = swap(cp, Z_ONE)
    vb = swap(va, Z_TWO)
    a = (va, 0)
    pq, sum_a = pair_sums([a], [(cp, 0), (cq, 0)], [None])
    cr, vb, pq = tie(cr, vb, pq)
    b = (vb, 0)
    v_far = swap(jnp.concatenate([va, vb], axis=0), Z_SIX)
    c, d = ((v_far, 0), (v_far, 4))
    cs = swap(cr, CORE)
    pqr, sum_b = pair_sums([b], [(cp, 0), (cq, 0), (cr, 0)], [None])
    s, sum_a, sum_b, sum_c, sum_d = pair_sums(
        [a, b, c, d], [(cs, 0)], [sum_a, sum_b, None, None]
    )
    s_back = swap(s, CORE)
    r, sum_a, sum_c, sum_d = pair_sums([a, c, d], [(cr, 0)], [sum_a, sum_c, sum_d], [(pqr, 8)])
    r = r + s_back
    r_back = swap(r, Z_ONE)
    r, pq = tie(r, pq)
    q, sum_c, sum_d = pair_sums([c, d], [(cq, 0)], [sum_c, sum_d], [(pq, 4), (pqr, 4)])
    q_back = swap(q, CORE)
    p, sum_d = pair_sums([d], [(cp, 0)], [sum_d], [(pq, 0), (pqr, 0)])
    bd_back = swap(jnp.concatenate([sum_b, sum_d], axis=0), Z_TWO)
    p, sum_c = pair_sums([c], [(cp, 0)], [sum_c], [(p, 0)])
    p, sum_c, bd_back, q_back, r_back = tie(p, sum_c, bd_back, q_back, r_back)
    p = p + q_back + r_back
    ctl_0, (ctl_1, ctl_2, ctl_3), sum_a, sum_c = tie(
        p[0],
        back(p, Y_MASKS),
        sum_a + bd_back[:4],
        swap(sum_c + bd_back[4:], Z_SIX),
    )
    vol = sum_a + sum_c
    vol_1, vol_2, vol_3 = back(vol, X_MASKS)
    ctl = (ctl_0 + ctl_1) + (ctl_2 + ctl_3)
    vol = (vol[0] + vol_1) + (vol_2 + vol_3)
    return (ctl[0:48], vol[0:3], ctl[48:51])


def solution(mesh):
    in_specs = (
        P(None, ("vol", "ctl")),
        P(None, ("vol", "ctl")),
        P(None, ("ctl", "vol")),
        P(None, ("ctl", "vol")),
    )
    out_specs = (P(None, ("ctl", "vol")), P(None, ("vol", "ctl")), P(None, ("ctl", "vol")))
    return jax.shard_map(shards, mesh=mesh, in_specs=in_specs, out_specs=out_specs, check_vma=False)
```

profile of v0, /device:TPU:8, one launch (start us, length us, event | category | flops | bytes accessed | tf_op | source)
XLA Modules:
  0.0 100.1 jit_solution(10017917433538275537)
XLA Ops:
  0.6 1.4 %shard_map.67 = (bf16[1,64,256]{2,1,0:T(8,128)(2,1)}, bf16[1,64,256]{2,1,0:T(8,128)(2,1)}) custom-call(bf16[3,256]{1,0:T(4,128)(2,1)} %vx_ref.1, bf16[48,256]{1,0:T(8,128)(2,1)} %vc_ref.1, bf16[3,256]{1,0:T(4,128)(2,1)} %cx_ref.1, bf16[48,256]{1,0:T(8,128)(2,1)} %cw_ref.1), custom_call_target="tpu_custom_call" | custom-call | tf_op jit(solution)/shard_map/pallas_call | solution.py:41
  2.1 2.3 %collective-permute-start.2 = (bf16[1,64,256]{2,1,0:T(8,128)(2,1)}, bf16[1,64,256]{2,1,0:T(8,128)(2,1)S(1)}, u32[]{:S(2)}, u32[]{:S(2)}) collective-permute-start(bf16[1,64,256]{2,1,0:T(8,128)(2,1)} %get-tuple-element.42), channel_id=1, source_target_pairs={{0,128},{1,129},{2,130},{3,131},{4,132},{5,133},{6,134},{7,135},{8... | collective-permute-start | bytes 98312 | tf_op jit(solution)/shard_map/ppermute | solution.py:146
  4.4 1.4 %collective-permute-start.1 = (bf16[1,64,256]{2,1,0:T(8,128)(2,1)}, bf16[1,64,256]{2,1,0:T(8,128)(2,1)S(1)}, u32[]{:S(2)}, u32[]{:S(2)}) collective-permute-start(bf16[1,64,256]{2,1,0:T(8,128)(2,1)} %get-tuple-element.42), channel_id=1, source_target_pairs={{0,192},{1,193},{2,194},{3,195},{4,196},{5,197},{6,198},{7,199},{8... | collective-permute-start | bytes 98312 | tf_op jit(solution)/shard_map/ppermute | solution.py:146
  5.7 1.1 %collective-permute-start = (bf16[1,64,256]{2,1,0:T(8,128)(2,1)}, bf16[1,64,256]{2,1,0:T(8,128)(2,1)S(1)}, u32[]{:S(2)}, u32[]{:S(2)}) collective-permute-start(bf16[1,64,256]{2,1,0:T(8,128)(2,1)} %get-tuple-element.42), channel_id=1, source_target_pairs={{0,64},{1,65},{2,66},{3,67},{4,68},{5,69},{6,70},{7,71},{8,72},{9,... | collective-permute-start | bytes 98312 | tf_op jit(solution)/shard_map/ppermute | solution.py:146
  6.8 3.0 %collective-permute-start.5 = (bf16[1,64,256]{2,1,0:T(8,128)(2,1)}, bf16[1,64,256]{2,1,0:T(8,128)(2,1)S(1)}, u32[]{:S(2)}, u32[]{:S(2)}) collective-permute-start(bf16[1,64,256]{2,1,0:T(8,128)(2,1)} %get-tuple-element.43), channel_id=1, source_target_pairs={{0,8},{1,9},{2,10},{3,11},{4,12},{5,13},{6,14},{7,15},{8,0},{9,1},... | collective-permute-start | bytes 98312 | tf_op jit(solution)/shard_map/ppermute | solution.py:146
  9.8 1.1 %collective-permute-start.4 = (bf16[1,64,256]{2,1,0:T(8,128)(2,1)}, bf16[1,64,256]{2,1,0:T(8,128)(2,1)S(1)}, u32[]{:S(2)}, u32[]{:S(2)}) collective-permute-start(bf16[1,64,256]{2,1,0:T(8,128)(2,1)} %get-tuple-element.43), channel_id=1, source_target_pairs={{0,12},{1,13},{2,14},{3,15},{4,8},{5,9},{6,10},{7,11},{8,4},{9,5},... | collective-permute-start | bytes 98312 | tf_op jit(solution)/shard_map/ppermute | solution.py:146
  11.0 0.8 pad_maximum_fusion.1.refs_1_
  11.7 0.7 collective-permute-done.5
  12.4 2.7 %collective-permute-done.4 = bf16[1,64,256]{2,1,0:T(8,128)(2,1)S(1)} collective-permute-done((bf16[1,64,256]{2,1,0:T(8,128)(2,1)}, bf16[1,64,256]{2,1,0:T(8,128)(2,1)S(1)}, u32[]{:S(2)}, u32[]{:S(2)}) %collective-permute-start.4) | collective-permute-done | bytes 32800 | tf_op jit(solution)/shard_map/ppermute | solution.py:146
  15.3 2.0 %collective-permute-start.6 = (bf16[4,64,256]{2,1,0:T(8,128)(2,1)S(1)}, bf16[4,64,256]{2,1,0:T(8,128)(2,1)S(1)}, u32[]{:S(2)}, u32[]{:S(2)}) collective-permute-start(bf16[4,64,256]{2,1,0:T(8,128)(2,1)S(1)} %pad_maximum_fusion.1.refs_1_), channel_id=1, source_target_pairs={{0,1},{1,0},{2,3},{3,2},{4,5},{5,4},{6,7},{7,6},{8,9},{9,8},{10,11... | collective-permute-start | bytes 393224 | tf_op jit(solution)/shard_map/ppermute | solution.py:146
  17.3 3.3 %collective-permute-start.7 = (bf16[4,64,256]{2,1,0:T(8,128)(2,1)S(1)}, bf16[4,64,256]{2,1,0:T(8,128)(2,1)S(1)}, u32[]{:S(2)}, u32[]{:S(2)}) collective-permute-start(bf16[4,64,256]{2,1,0:T(8,128)(2,1)S(1)} %pad_maximum_fusion.2.refs_0_), channel_id=1, source_target_pairs={{0,2},{1,3},{2,0},{3,1},{4,6},{5,7},{6,4},{7,5},{8,10},{9,11},{10,... | collective-permute-start | bytes 393224 | tf_op jit(solution)/shard_map/ppermute | solution.py:146
  20.5 6.4 %shard_map.68 = (f32[8,56,256]{2,1,0:T(8,128)S(1)}, f32[4,8,256]{2,1,0:T(8,128)S(1)}) custom-call(bf16[4,64,256]{2,1,0:T(8,128)(2,1)S(1)} %pad_maximum_fusion.2.refs_0_, bf16[4,64,256]{2,1,0:T(8,128)(2,1)S(1)} %pad_maximum_fusion.1.refs_1_, bf16[4,64,256]{2,1,0:T(8,128)(2,1)S(1)} %collective-permute-done.8.refs_2_), custom_call_target="tpu_custom_call" | custom-call | flops 6400000000 | bytes 4000000 | tf_op jit(solution)/shard_map/pallas_call | solution.py:124
  27.2 3.8 %collective-permute-start.9 = (bf16[8,64,256]{2,1,0:T(8,128)(2,1)S(1)}, bf16[8,64,256]{2,1,0:T(8,128)(2,1)S(1)}, u32[]{:S(2)}, u32[]{:S(2)}) collective-permute-start(bf16[8,64,256]{2,1,0:T(8,128)(2,1)S(1)} %pad_maximum_fusion), channel_id=1, source_target_pairs={{0,34},{1,35},{2,32},{3,33},{4,38},{5,39},{6,36},{7,37},{8,42},{9,... | collective-permute-start | bytes 786440 | tf_op jit(solution)/shard_map/ppermute | solution.py:146
  31.0 9.6 %shard_map.69 = (f32[12,56,256]{2,1,0:T(8,128)S(1)}, f32[4,8,256]{2,1,0:T(8,128)S(1)}) custom-call(bf16[4,64,256]{2,1,0:T(8,128)(2,1)S(1)} %collective-permute-done.7.refs_0_.refs_1_, bf16[4,64,256]{2,1,0:T(8,128)(2,1)S(1)} %pad_maximum_fusion.1.refs_1_, bf16[4,64,256]{2,1,0:T(8,128)(2,1)S(1)} %collective-permute-done.8.refs_2_, ...), custom_call_target="tpu_custom_call" | custom-call | flops 9600000000 | bytes 4000000 | tf_op jit(solution)/shard_map/pallas_call | solution.py:124
  40.6 2.2 %collective-permute-done.9.refs_2_.refs_3_.refs_1_.refs_0_ = bf16[8,64,256]{2,1,0:T(8,128)(2,1)S(1)} collective-permute-done((bf16[8,64,256]{2,1,0:T(8,128)(2,1)S(1)}, bf16[8,64,256]{2,1,0:T(8,128)(2,1)S(1)}, u32[]{:S(2)}, u32[]{:S(2)}) %collective-permute-start.9) | collective-permute-done | bytes 262176 | tf_op jit(solution)/shard_map/ppermute | solution.py:146
  42.8 11.7 %shard_map.70 = (f32[4,56,256]{2,1,0:T(8,128)S(1)}, f32[4,8,256]{2,1,0:T(8,128)S(1)}, f32[4,8,256]{2,1,0:T(8,128)S(1)}, f32[4,8,256]{2,1,0:T(8,128)S(1)}, f32[4,8,256]{2,1,0:T(8,128)S(1)}) custom-call(bf16[4,64,256]{2,1,0:T(8,128)(2,1)S(1)} %pad_maximum_fusion.2.refs_0_, bf16[4,64,256]{2,1,0:T(8,128)(2,1)S(1)} %collective-permute-done.7.refs_0_.refs_1_, ...), custom_call_target="tpu_custom_call" | custom-call | flops 12800000000 | bytes 4000000 | tf_op jit(solution)/shard_map/pallas_call | solution.py:124
  54.8 9.0 %shard_map.71 = (f32[4,56,256]{2,1,0:T(8,128)S(1)}, f32[4,8,256]{2,1,0:T(8,128)S(1)}, f32[4,8,256]{2,1,0:T(8,128)S(1)}, f32[4,8,256]{2,1,0:T(8,128)S(1)}) custom-call(bf16[4,64,256]{2,1,0:T(8,128)(2,1)S(1)} %pad_maximum_fusion.2.refs_0_, bf16[8,64,256]{2,1,0:T(8,128)(2,1)S(1)} %collective-permute-done.9.refs_2_.refs_3_.refs_1_.refs_0_, ...), custom_call_target="tpu_custom_call" | custom-call | flops 9600000000 | bytes 4000000 | tf_op jit(solution)/shard_map/pallas_call | solution.py:124
  63.8 2.6 %collective-permute-start.14 = (f32[4,56,256]{2,1,0:T(8,128)S(1)}, f32[4,56,256]{2,1,0:T(8,128)S(1)}, u32[]{:S(2)}, u32[]{:S(2)}) collective-permute-start(f32[4,56,256]{2,1,0:T(8,128)S(1)} %add.36), channel_id=1, source_target_pairs={{0,1},{1,0},{2,3},{3,2},{4,5},{5,4},{6,7},{7,6},{8,9},{9,8},{10,11... | collective-permute-start | bytes 688136 | tf_op jit(solution)/shard_map/ppermute | solution.py:146
  66.4 6.0 %shard_map.72 = (f32[4,56,256]{2,1,0:T(8,128)S(1)}, f32[4,8,256]{2,1,0:T(8,128)S(1)}, f32[4,8,256]{2,1,0:T(8,128)S(1)}) custom-call(bf16[8,64,256]{2,1,0:T(8,128)(2,1)S(1)} %collective-permute-done.9.refs_2_.refs_3_.refs_1_.refs_0_, bf16[8,64,256]{2,1,0:T(8,128)(2,1)S(1)} %collective-permute-done.9.refs_2_.refs_3_.refs_1_.refs_0_, ...), custom_call_target="tpu_custom_call" | custom-call | flops 6400000000 | bytes 4000000 | tf_op jit(solution)/shard_map/pallas_call | solution.py:124
  72.5 3.3 %shard_map.73 = (f32[4,56,256]{2,1,0:T(8,128)S(1)}, f32[4,8,256]{2,1,0:T(8,128)S(1)}) custom-call(bf16[8,64,256]{2,1,0:T(8,128)(2,1)S(1)} %collective-permute-done.9.refs_2_.refs_3_.refs_1_.refs_0_, bf16[4,64,256]{2,1,0:T(8,128)(2,1)S(1)} %pad_maximum_fusion.1.refs_1_, f32[8,56,256]{2,1,0:T(8,128)S(1)} %get-tuple-element.58.refs_3_.refs_2_, ...), custom_call_target="tpu_custom_call" | custom-call | flops 3200000000 | bytes 4000000 | tf_op jit(solution)/shard_map/pallas_call | solution.py:124
  75.8 1.0 %collective-permute-start.12 = (f32[8,8,256]{2,1,0:T(8,128)S(1)}, f32[8,8,256]{2,1,0:T(8,128)S(1)}, u32[]{:S(2)}, u32[]{:S(2)}) collective-permute-start(f32[8,8,256]{2,1,0:T(8,128)S(1)} %pad_maximum_fusion.3), channel_id=1, source_target_pairs={{0,2},{1,3},{2,0},{3,1},{4,6},{5,7},{6,4},{7,5},{8,10},{9,11},{10,... | collective-permute-start | bytes 196616 | tf_op jit(solution)/shard_map/ppermute | solution.py:146
  76.9 3.3 %shard_map.74 = (f32[4,56,256]{2,1,0:T(8,128)S(1)}, f32[4,8,256]{2,1,0:T(8,128)S(1)}) custom-call(bf16[8,64,256]{2,1,0:T(8,128)(2,1)S(1)} %collective-permute-done.9.refs_2_.refs_3_.refs_1_.refs_0_, bf16[4,64,256]{2,1,0:T(8,128)(2,1)S(1)} %pad_maximum_fusion.1.refs_1_, f32[4,56,256]{2,1,0:T(8,128)S(1)} %get-tuple-element.62.refs_2_, ...), custom_call_target="tpu_custom_call" | custom-call | flops 3200000000 | bytes 4000000 | tf_op jit(solution)/shard_map/pallas_call | solution.py:124
  80.2 1.8 %collective-permute-done.12 = f32[8,8,256]{2,1,0:T(8,128)S(1)} collective-permute-done((f32[8,8,256]{2,1,0:T(8,128)S(1)}, f32[8,8,256]{2,1,0:T(8,128)S(1)}, u32[]{:S(2)}, u32[]{:S(2)}) %collective-permute-start.12) | collective-permute-done | bytes 65568 | tf_op jit(solution)/shard_map/ppermute | solution.py:146
  82.1 1.2 %collective-permute-start.17 = (f32[56,256]{1,0:T(8,128)S(1)}, f32[56,256]{1,0:T(8,128)S(1)}, u32[]{:S(2)}, u32[]{:S(2)}) collective-permute-start(f32[56,256]{1,0:T(8,128)S(1)} %get-tuple-element.81), channel_id=1, source_target_pairs={{0,128},{1,129},{2,130},{3,131},{4,132},{5,133},{6,134},{7,135},{8... | collective-permute-start | bytes 172040 | tf_op jit(solution)/shard_map/ppermute | solution.py:146
  83.9 3.0 %collective-permute-start.15 = (f32[56,256]{1,0:T(8,128)S(1)}, f32[56,256]{1,0:T(8,128)S(1)}, u32[]{:S(2)}, u32[]{:S(2)}) collective-permute-start(f32[56,256]{1,0:T(8,128)S(1)} %get-tuple-element.83), channel_id=1, source_target_pairs={{0,64},{1,65},{2,66},{3,67},{4,68},{5,69},{6,70},{7,71},{8,72},{9,... | collective-permute-start | bytes 172040 | tf_op jit(solution)/shard_map/ppermute | solution.py:146
  86.9 1.8 %collective-permute-start.18 = (f32[4,8,256]{2,1,0:T(8,128)S(1)}, f32[4,8,256]{2,1,0:T(8,128)S(1)}, u32[]{:S(2)}, u32[]{:S(2)}) collective-permute-start(f32[4,8,256]{2,1,0:T(8,128)S(1)} %get-tuple-element.85), channel_id=1, source_target_pairs={{0,34},{1,35},{2,32},{3,33},{4,38},{5,39},{6,36},{7,37},{8,42},{9,... | collective-permute-start | bytes 98312 | tf_op jit(solution)/shard_map/ppermute | solution.py:146
  88.7 4.3 %collective-permute-done.18 = f32[4,8,256]{2,1,0:T(8,128)S(1)} collective-permute-done((f32[4,8,256]{2,1,0:T(8,128)S(1)}, f32[4,8,256]{2,1,0:T(8,128)S(1)}, u32[]{:S(2)}, u32[]{:S(2)}) %collective-permute-start.18) | collective-permute-done | bytes 32800 | tf_op jit(solution)/shard_map/ppermute | solution.py:146
  93.0 1.6 %collective-permute-start.21 = (f32[8,256]{1,0:T(8,128)S(1)}, f32[8,256]{1,0:T(8,128)S(1)}, u32[]{:S(2)}, u32[]{:S(2)}) collective-permute-start(f32[8,256]{1,0:T(8,128)S(1)} %get-tuple-element.88), channel_id=1, source_target_pairs={{0,8},{1,9},{2,10},{3,11},{4,12},{5,13},{6,14},{7,15},{8,0},{9,1},... | collective-permute-start | bytes 24584 | tf_op jit(solution)/shard_map/ppermute | solution.py:146
  94.7 1.1 %collective-permute-start.20 = (f32[8,256]{1,0:T(8,128)S(1)}, f32[8,256]{1,0:T(8,128)S(1)}, u32[]{:S(2)}, u32[]{:S(2)}) collective-permute-start(f32[8,256]{1,0:T(8,128)S(1)} %get-tuple-element.89), channel_id=1, source_target_pairs={{0,12},{1,13},{2,14},{3,15},{4,8},{5,9},{6,10},{7,11},{8,4},{9,5},... | collective-permute-start | bytes 24584 | tf_op jit(solution)/shard_map/ppermute | solution.py:146
  95.8 0.8 collective-permute-start.19
  97.2 0.6 slice.56
  98.3 1.2 %collective-permute-done.20 = f32[8,256]{1,0:T(8,128)S(1)} collective-permute-done((f32[8,256]{1,0:T(8,128)S(1)}, f32[8,256]{1,0:T(8,128)S(1)}, u32[]{:S(2)}, u32[]{:S(2)}) %collective-permute-start.20) | collective-permute-done | bytes 8224 | tf_op jit(solution)/shard_map/ppermute | solution.py:146
  (36 shorter events, 3.0 us)
Async XLA Ops:
  2.1 8.9 %collective-permute-start.2 = (bf16[1,64,256]{2,1,0:T(8,128)(2,1)}, bf16[1,64,256]{2,1,0:T(8,128)(2,1)S(1)}, u32[]{:S(2)}, u32[]{:S(2)}) collective-permute-start(bf16[1,64,256]{2,1,0:T(8,128)(2,1)} %get-tuple-element.42), channel_id=1, source_target_pairs={{0,128},{1,129},{2,130},{3,131},{4,132},{5,133},{6,134},{7,135},{8... | collective-permute-start | bytes 98312 | tf_op jit(solution)/shard_map/ppermute | solution.py:146
  4.4 6.6 %collective-permute-start.1 = (bf16[1,64,256]{2,1,0:T(8,128)(2,1)}, bf16[1,64,256]{2,1,0:T(8,128)(2,1)S(1)}, u32[]{:S(2)}, u32[]{:S(2)}) collective-permute-start(bf16[1,64,256]{2,1,0:T(8,128)(2,1)} %get-tuple-element.42), channel_id=1, source_target_pairs={{0,192},{1,193},{2,194},{3,195},{4,196},{5,197},{6,198},{7,199},{8... | collective-permute-start | bytes 98312 | tf_op jit(solution)/shard_map/ppermute | solution.py:146
  5.7 5.2 %collective-permute-start = (bf16[1,64,256]{2,1,0:T(8,128)(2,1)}, bf16[1,64,256]{2,1,0:T(8,128)(2,1)S(1)}, u32[]{:S(2)}, u32[]{:S(2)}) collective-permute-start(bf16[1,64,256]{2,1,0:T(8,128)(2,1)} %get-tuple-element.42), channel_id=1, source_target_pairs={{0,64},{1,65},{2,66},{3,67},{4,68},{5,69},{6,70},{7,71},{8,72},{9,... | collective-permute-start | bytes 98312 | tf_op jit(solution)/shard_map/ppermute | solution.py:146
  6.8 8.4 %copy-start = (bf16[1,64,256]{2,1,0:T(8,128)(2,1)S(1)}, bf16[1,64,256]{2,1,0:T(8,128)(2,1)}, u32[]{:S(2)}) copy-start(bf16[1,64,256]{2,1,0:T(8,128)(2,1)} %get-tuple-element.43) | copy-start | bytes 98308
  6.8 5.6 %collective-permute-start.5 = (bf16[1,64,256]{2,1,0:T(8,128)(2,1)}, bf16[1,64,256]{2,1,0:T(8,128)(2,1)S(1)}, u32[]{:S(2)}, u32[]{:S(2)}) collective-permute-start(bf16[1,64,256]{2,1,0:T(8,128)(2,1)} %get-tuple-element.43), channel_id=1, source_target_pairs={{0,8},{1,9},{2,10},{3,11},{4,12},{5,13},{6,14},{7,15},{8,0},{9,1},... | collective-permute-start | bytes 98312 | tf_op jit(solution)/shard_map/ppermute | solution.py:146
  9.8 5.3 %collective-permute-start.4 = (bf16[1,64,256]{2,1,0:T(8,128)(2,1)}, bf16[1,64,256]{2,1,0:T(8,128)(2,1)S(1)}, u32[]{:S(2)}, u32[]{:S(2)}) collective-permute-start(bf16[1,64,256]{2,1,0:T(8,128)(2,1)} %get-tuple-element.43), channel_id=1, source_target_pairs={{0,12},{1,13},{2,14},{3,15},{4,8},{5,9},{6,10},{7,11},{8,4},{9,5},... | collective-permute-start | bytes 98312 | tf_op jit(solution)/shard_map/ppermute | solution.py:146
  10.9 4.2 %collective-permute-start.3 = (bf16[1,64,256]{2,1,0:T(8,128)(2,1)}, bf16[1,64,256]{2,1,0:T(8,128)(2,1)S(1)}, u32[]{:S(2)}, u32[]{:S(2)}) collective-permute-start(bf16[1,64,256]{2,1,0:T(8,128)(2,1)} %get-tuple-element.43), channel_id=1, source_target_pairs={{0,4},{1,5},{2,6},{3,7},{4,0},{5,1},{6,2},{7,3},{8,12},{9,13},{10,... | collective-permute-start | bytes 98312 | tf_op jit(solution)/shard_map/ppermute | solution.py:146
  15.2 5.4 %collective-permute-start.8 = (bf16[4,64,256]{2,1,0:T(8,128)(2,1)S(1)}, bf16[4,64,256]{2,1,0:T(8,128)(2,1)S(1)}, u32[]{:S(2)}, u32[]{:S(2)}) collective-permute-start(bf16[4,64,256]{2,1,0:T(8,128)(2,1)S(1)} %pad_maximum_fusion.1.refs_1_), channel_id=1, source_target_pairs={{0,16},{1,17},{2,18},{3,19},{4,20},{5,21},{6,22},{7,23},{8,24},{9,... | collective-permute-start | bytes 393224 | tf_op jit(solution)/shard_map/ppermute | solution.py:146
  15.3 11.9 %collective-permute-start.6 = (bf16[4,64,256]{2,1,0:T(8,128)(2,1)S(1)}, bf16[4,64,256]{2,1,0:T(8,128)(2,1)S(1)}, u32[]{:S(2)}, u32[]{:S(2)}) collective-permute-start(bf16[4,64,256]{2,1,0:T(8,128)(2,1)S(1)} %pad_maximum_fusion.1.refs_1_), channel_id=1, source_target_pairs={{0,1},{1,0},{2,3},{3,2},{4,5},{5,4},{6,7},{7,6},{8,9},{9,8},{10,11... | collective-permute-start | bytes 393224 | tf_op jit(solution)/shard_map/ppermute | solution.py:146
  17.3 9.9 %collective-permute-start.7 = (bf16[4,64,256]{2,1,0:T(8,128)(2,1)S(1)}, bf16[4,64,256]{2,1,0:T(8,128)(2,1)S(1)}, u32[]{:S(2)}, u32[]{:S(2)}) collective-permute-start(bf16[4,64,256]{2,1,0:T(8,128)(2,1)S(1)} %pad_maximum_fusion.2.refs_0_), channel_id=1, source_target_pairs={{0,2},{1,3},{2,0},{3,1},{4,6},{5,7},{6,4},{7,5},{8,10},{9,11},{10,... | collective-permute-start | bytes 393224 | tf_op jit(solution)/shard_map/ppermute | solution.py:146
  27.2 13.4 %collective-permute-start.10 = (bf16[4,64,256]{2,1,0:T(8,128)(2,1)S(1)}, bf16[4,64,256]{2,1,0:T(8,128)(2,1)S(1)}, u32[]{:S(2)}, u32[]{:S(2)}) collective-permute-start(bf16[4,64,256]{2,1,0:T(8,128)(2,1)S(1)} %collective-permute-done.6.refs_3_), channel_id=1, source_target_pairs={{0,16},{1,17},{2,18},{3,19},{4,20},{5,21},{6,22},{7,23},{8,24},{9,... | collective-permute-start | bytes 393224 | tf_op jit(solution)/shard_map/ppermute | solution.py:146
  27.2 15.6 %collective-permute-start.9 = (bf16[8,64,256]{2,1,0:T(8,128)(2,1)S(1)}, bf16[8,64,256]{2,1,0:T(8,128)(2,1)S(1)}, u32[]{:S(2)}, u32[]{:S(2)}) collective-permute-start(bf16[8,64,256]{2,1,0:T(8,128)(2,1)S(1)} %pad_maximum_fusion), channel_id=1, source_target_pairs={{0,34},{1,35},{2,32},{3,33},{4,38},{5,39},{6,36},{7,37},{8,42},{9,... | collective-permute-start | bytes 786440 | tf_op jit(solution)/shard_map/ppermute | solution.py:146
  54.5 9.3 %collective-permute-start.11 = (f32[4,56,256]{2,1,0:T(8,128)S(1)}, f32[4,56,256]{2,1,0:T(8,128)S(1)}, u32[]{:S(2)}, u32[]{:S(2)}) collective-permute-start(f32[4,56,256]{2,1,0:T(8,128)S(1)} %get-tuple-element.56), channel_id=1, source_target_pairs={{0,16},{1,17},{2,18},{3,19},{4,20},{5,21},{6,22},{7,23},{8,24},{9,... | collective-permute-start | bytes 688136 | tf_op jit(solution)/shard_map/ppermute | solution.py:146
  63.8 18.2 %collective-permute-start.14 = (f32[4,56,256]{2,1,0:T(8,128)S(1)}, f32[4,56,256]{2,1,0:T(8,128)S(1)}, u32[]{:S(2)}, u32[]{:S(2)}) collective-permute-start(f32[4,56,256]{2,1,0:T(8,128)S(1)} %add.36), channel_id=1, source_target_pairs={{0,1},{1,0},{2,3},{3,2},{4,5},{5,4},{6,7},{7,6},{8,9},{9,8},{10,11... | collective-permute-start | bytes 688136 | tf_op jit(solution)/shard_map/ppermute | solution.py:146
  75.8 6.2 %collective-permute-start.12 = (f32[8,8,256]{2,1,0:T(8,128)S(1)}, f32[8,8,256]{2,1,0:T(8,128)S(1)}, u32[]{:S(2)}, u32[]{:S(2)}) collective-permute-start(f32[8,8,256]{2,1,0:T(8,128)S(1)} %pad_maximum_fusion.3), channel_id=1, source_target_pairs={{0,2},{1,3},{2,0},{3,1},{4,6},{5,7},{6,4},{7,5},{8,10},{9,11},{10,... | collective-permute-start | bytes 196616 | tf_op jit(solution)/shard_map/ppermute | solution.py:146
  76.8 5.2 %collective-permute-start.13 = (f32[4,56,256]{2,1,0:T(8,128)S(1)}, f32[4,56,256]{2,1,0:T(8,128)S(1)}, u32[]{:S(2)}, u32[]{:S(2)}) collective-permute-start(f32[4,56,256]{2,1,0:T(8,128)S(1)} %get-tuple-element.68), channel_id=1, source_target_pairs={{0,16},{1,17},{2,18},{3,19},{4,20},{5,21},{6,22},{7,23},{8,24},{9,... | collective-permute-start | bytes 688136 | tf_op jit(solution)/shard_map/ppermute | solution.py:146
  82.1 10.9 %collective-permute-start.17 = (f32[56,256]{1,0:T(8,128)S(1)}, f32[56,256]{1,0:T(8,128)S(1)}, u32[]{:S(2)}, u32[]{:S(2)}) collective-permute-start(f32[56,256]{1,0:T(8,128)S(1)} %get-tuple-element.81), channel_id=1, source_target_pairs={{0,128},{1,129},{2,130},{3,131},{4,132},{5,133},{6,134},{7,135},{8... | collective-permute-start | bytes 172040 | tf_op jit(solution)/shard_map/ppermute | solution.py:146
  83.3 9.7 %collective-permute-start.16 = (f32[56,256]{1,0:T(8,128)S(1)}, f32[56,256]{1,0:T(8,128)S(1)}, u32[]{:S(2)}, u32[]{:S(2)}) collective-permute-start(f32[56,256]{1,0:T(8,128)S(1)} %get-tuple-element.82), channel_id=1, source_target_pairs={{0,192},{1,193},{2,194},{3,195},{4,196},{5,197},{6,198},{7,199},{8... | collective-permute-start | bytes 172040 | tf_op jit(solution)/shard_map/ppermute | solution.py:146
  83.9 9.1 %collective-permute-start.15 = (f32[56,256]{1,0:T(8,128)S(1)}, f32[56,256]{1,0:T(8,128)S(1)}, u32[]{:S(2)}, u32[]{:S(2)}) collective-permute-start(f32[56,256]{1,0:T(8,128)S(1)} %get-tuple-element.83), channel_id=1, source_target_pairs={{0,64},{1,65},{2,66},{3,67},{4,68},{5,69},{6,70},{7,71},{8,72},{9,... | collective-permute-start | bytes 172040 | tf_op jit(solution)/shard_map/ppermute | solution.py:146
  86.9 6.1 %collective-permute-start.18 = (f32[4,8,256]{2,1,0:T(8,128)S(1)}, f32[4,8,256]{2,1,0:T(8,128)S(1)}, u32[]{:S(2)}, u32[]{:S(2)}) collective-permute-start(f32[4,8,256]{2,1,0:T(8,128)S(1)} %get-tuple-element.85), channel_id=1, source_target_pairs={{0,34},{1,35},{2,32},{3,33},{4,38},{5,39},{6,36},{7,37},{8,42},{9,... | collective-permute-start | bytes 98312 | tf_op jit(solution)/shard_map/ppermute | solution.py:146
  93.0 5.2 %collective-permute-start.21 = (f32[8,256]{1,0:T(8,128)S(1)}, f32[8,256]{1,0:T(8,128)S(1)}, u32[]{:S(2)}, u32[]{:S(2)}) collective-permute-start(f32[8,256]{1,0:T(8,128)S(1)} %get-tuple-element.88), channel_id=1, source_target_pairs={{0,8},{1,9},{2,10},{3,11},{4,12},{5,13},{6,14},{7,15},{8,0},{9,1},... | collective-permute-start | bytes 24584 | tf_op jit(solution)/shard_map/ppermute | solution.py:146
  94.7 4.9 %collective-permute-start.20 = (f32[8,256]{1,0:T(8,128)S(1)}, f32[8,256]{1,0:T(8,128)S(1)}, u32[]{:S(2)}, u32[]{:S(2)}) collective-permute-start(f32[8,256]{1,0:T(8,128)S(1)} %get-tuple-element.89), channel_id=1, source_target_pairs={{0,12},{1,13},{2,14},{3,15},{4,8},{5,9},{6,10},{7,11},{8,4},{9,5},... | collective-permute-start | bytes 24584 | tf_op jit(solution)/shard_map/ppermute | solution.py:146
  95.8 3.7 %collective-permute-start.19 = (f32[8,256]{1,0:T(8,128)S(1)}, f32[8,256]{1,0:T(8,128)S(1)}, u32[]{:S(2)}, u32[]{:S(2)}) collective-permute-start(f32[8,256]{1,0:T(8,128)S(1)} %get-tuple-element.90), channel_id=1, source_target_pairs={{0,4},{1,5},{2,6},{3,7},{4,0},{5,1},{6,2},{7,3},{8,12},{9,13},{10,... | collective-permute-start | bytes 24584 | tf_op jit(solution)/shard_map/ppermute | solution.py:146
where the time goes:
time: 100 us
  Pallas kernels  50.8 us (51%)
  starting transfers between devices  32.2 us (32%)
  waiting for transfers between devices  13.6 us (14%)
  other arithmetic  1.53 us (2%)
  local copies, waits for them, and re-layouts  1.25 us (1%)
    pallas_call x7, Pallas kernels, pair_sums(): pl.pallas_call(body, out_shape=[jax.ShapeDtypeStruct((c_count, 56, BLOCK)...  49.3 us
    ppermute x22, starting transfers between devices, swap(): lax.ppermute(value, ('vol', 'ctl'), [(i, i ^ mask) for i in range(256)])  32.2 us
    ppermute x22, waiting for transfers between devices, swap(): lax.ppermute(value, ('vol', 'ctl'), [(i, i ^ mask) for i in range(256)])  13.6 us
  transfers between devices with their start and end apart: 22, of which 8 were waited for; matrix products, arithmetic and copies ran while one was open for 2% of the time, Pallas kernels for 38%

commit v1 on v0

--- a/solution.py
+++ b/solution.py
@@ -193,16 +193,11 @@
     p, sum_c = pair_sums([c], [(cp, 0)], [sum_c], [(p, 0)])
     p, sum_c, bd_back, q_back, r_back = tie(p, sum_c, bd_back, q_back, r_back)
     p = p + q_back + r_back
-    ctl_0, (ctl_1, ctl_2, ctl_3), sum_a, sum_c = tie(
-        p[0],
-        back(p, Y_MASKS),
-        sum_a + bd_back[:4],
-        swap(sum_c + bd_back[4:], Z_SIX),
-    )
-    vol = sum_a + sum_c
-    vol_1, vol_2, vol_3 = back(vol, X_MASKS)
-    ctl = (ctl_0 + ctl_1) + (ctl_2 + ctl_3)
-    vol = (vol[0] + vol_1) + (vol_2 + vol_3)
+    vol = sum_a + bd_back[:4] + swap(sum_c + bd_back[4:], Z_SIX)
+    ctl, vol = tie([p[0], *back(p.astype(BF), Y_MASKS)], [vol[0], *back(vol, X_MASKS)])
+    ctl = [term.astype(F32) for term in ctl]
+    ctl = (ctl[0] + ctl[1]) + (ctl[2] + ctl[3])
+    vol = (vol[0] + vol[1]) + (vol[2] + vol[3])
     return (ctl[0:48], vol[0:3], ctl[48:51])
 
 

time: 100 us -> 97.8 us (0.978)
  waiting for transfers between devices: 13.6 us -> 10.5 us
    ppermute x22, waiting for transfers between devices: 13.6 us -> 10.5 us  [swap(): lax.ppermute(value, ('vol', 'ctl'), [(i, i ^ mask) for i in range(256)])]
  transfers between devices with their start and end apart: 22 -> 22, of which waited for: 8 -> 7; matrix products, arithmetic and copies ran while one was open for 2% -> 1% of each run, Pallas kernels for 38% -> 39%
where the time goes in v1:
time: 97.8 us; the launch traced here: 97 us
  Pallas kernels  50.8 us (52%)
  starting transfers between devices  32.2 us (33%)
  waiting for transfers between devices  10.5 us (11%)
  other arithmetic  1.53 us (2%)
  local copies, waits for them, and re-layouts  1.24 us (1%)
    pallas_call x7, Pallas kernels, pair_sums(): pl.pallas_call(body, out_shape=[jax.ShapeDtypeStruct((c_count, 56, BLOCK)...  49.3 us
    ppermute x22, starting transfers between devices, swap(): lax.ppermute(value, ('vol', 'ctl'), [(i, i ^ mask) for i in range(256)])  32.2 us
    ppermute x22, waiting for transfers between devices, swap(): lax.ppermute(value, ('vol', 'ctl'), [(i, i ^ mask) for i in range(256)])  10.5 us
  transfers between devices with their start and end apart: 22, of which 7 were waited for; matrix products, arithmetic and copies ran while one was open for 1% of the time, Pallas kernels for 39%

profile of v1, /device:TPU:8, one launch (start us, length us, event | category | flops | bytes accessed | tf_op | source)
XLA Modules:
  0.0 97.0 jit_solution(7300474843729252253)
XLA Ops:
  0.6 1.4 %shard_map.67 = (bf16[1,64,256]{2,1,0:T(8,128)(2,1)}, bf16[1,64,256]{2,1,0:T(8,128)(2,1)}) custom-call(bf16[3,256]{1,0:T(4,128)(2,1)} %vx_ref.1, bf16[48,256]{1,0:T(8,128)(2,1)} %vc_ref.1, bf16[3,256]{1,0:T(4,128)(2,1)} %cx_ref.1, bf16[48,256]{1,0:T(8,128)(2,1)} %cw_ref.1), custom_call_target="tpu_custom_call" | custom-call | tf_op jit(solution)/shard_map/pallas_call | solution.py:41
  2.1 2.3 %collective-permute-start.2 = (bf16[1,64,256]{2,1,0:T(8,128)(2,1)}, bf16[1,64,256]{2,1,0:T(8,128)(2,1)S(1)}, u32[]{:S(2)}, u32[]{:S(2)}) collective-permute-start(bf16[1,64,256]{2,1,0:T(8,128)(2,1)} %get-tuple-element.44), channel_id=1, source_target_pairs={{0,128},{1,129},{2,130},{3,131},{4,132},{5,133},{6,134},{7,135},{8... | collective-permute-start | bytes 98312 | tf_op jit(solution)/shard_map/ppermute | solution.py:146
  4.4 1.4 %collective-permute-start.1 = (bf16[1,64,256]{2,1,0:T(8,128)(2,1)}, bf16[1,64,256]{2,1,0:T(8,128)(2,1)S(1)}, u32[]{:S(2)}, u32[]{:S(2)}) collective-permute-start(bf16[1,64,256]{2,1,0:T(8,128)(2,1)} %get-tuple-element.44), channel_id=1, source_target_pairs={{0,192},{1,193},{2,194},{3,195},{4,196},{5,197},{6,198},{7,199},{8... | collective-permute-start | bytes 98312 | tf_op jit(solution)/shard_map/ppermute | solution.py:146
  5.7 1.1 %collective-permute-start = (bf16[1,64,256]{2,1,0:T(8,128)(2,1)}, bf16[1,64,256]{2,1,0:T(8,128)(2,1)S(1)}, u32[]{:S(2)}, u32[]{:S(2)}) collective-permute-start(bf16[1,64,256]{2,1,0:T(8,128)(2,1)} %get-tuple-element.44), channel_id=1, source_target_pairs={{0,64},{1,65},{2,66},{3,67},{4,68},{5,69},{6,70},{7,71},{8,72},{9,... | collective-permute-start | bytes 98312 | tf_op jit(solution)/shard_map/ppermute | solution.py:146
  6.8 3.0 %collective-permute-start.5 = (bf16[1,64,256]{2,1,0:T(8,128)(2,1)}, bf16[1,64,256]{2,1,0:T(8,128)(2,1)S(1)}, u32[]{:S(2)}, u32[]{:S(2)}) collective-permute-start(bf16[1,64,256]{2,1,0:T(8,128)(2,1)} %get-tuple-element.45), channel_id=1, source_target_pairs={{0,8},{1,9},{2,10},{3,11},{4,12},{5,13},{6,14},{7,15},{8,0},{9,1},... | collective-permute-start | bytes 98312 | tf_op jit(solution)/shard_map/ppermute | solution.py:146
  9.8 1.1 %collective-permute-start.4 = (bf16[1,64,256]{2,1,0:T(8,128)(2,1)}, bf16[1,64,256]{2,1,0:T(8,128)(2,1)S(1)}, u32[]{:S(2)}, u32[]{:S(2)}) collective-permute-start(bf16[1,64,256]{2,1,0:T(8,128)(2,1)} %get-tuple-element.45), channel_id=1, source_target_pairs={{0,12},{1,13},{2,14},{3,15},{4,8},{5,9},{6,10},{7,11},{8,4},{9,5},... | collective-permute-start | bytes 98312 | tf_op jit(solution)/shard_map/ppermute | solution.py:146
  11.0 0.8 pad_maximum_fusion.1.refs_1_
  11.7 0.7 collective-permute-done.5
  12.4 2.7 %collective-permute-done.4 = bf16[1,64,256]{2,1,0:T(8,128)(2,1)S(1)} collective-permute-done((bf16[1,64,256]{2,1,0:T(8,128)(2,1)}, bf16[1,64,256]{2,1,0:T(8,128)(2,1)S(1)}, u32[]{:S(2)}, u32[]{:S(2)}) %collective-permute-start.4) | collective-permute-done | bytes 32800 | tf_op jit(solution)/shard_map/ppermute | solution.py:146
  15.3 2.0 %collective-permute-start.6 = (bf16[4,64,256]{2,1,0:T(8,128)(2,1)S(1)}, bf16[4,64,256]{2,1,0:T(8,128)(2,1)S(1)}, u32[]{:S(2)}, u32[]{:S(2)}) collective-permute-start(bf16[4,64,256]{2,1,0:T(8,128)(2,1)S(1)} %pad_maximum_fusion.1.refs_1_), channel_id=1, source_target_pairs={{0,1},{1,0},{2,3},{3,2},{4,5},{5,4},{6,7},{7,6},{8,9},{9,8},{10,11... | collective-permute-start | bytes 393224 | tf_op jit(solution)/shard_map/ppermute | solution.py:146
  17.3 3.3 %collective-permute-start.7 = (bf16[4,64,256]{2,1,0:T(8,128)(2,1)S(1)}, bf16[4,64,256]{2,1,0:T(8,128)(2,1)S(1)}, u32[]{:S(2)}, u32[]{:S(2)}) collective-permute-start(bf16[4,64,256]{2,1,0:T(8,128)(2,1)S(1)} %pad_maximum_fusion.2.refs_0_), channel_id=1, source_target_pairs={{0,2},{1,3},{2,0},{3,1},{4,6},{5,7},{6,4},{7,5},{8,10},{9,11},{10,... | collective-permute-start | bytes 393224 | tf_op jit(solution)/shard_map/ppermute | solution.py:146
  20.5 6.4 %shard_map.68 = (f32[8,56,256]{2,1,0:T(8,128)S(1)}, f32[4,8,256]{2,1,0:T(8,128)S(1)}) custom-call(bf16[4,64,256]{2,1,0:T(8,128)(2,1)S(1)} %pad_maximum_fusion.2.refs_0_, bf16[4,64,256]{2,1,0:T(8,128)(2,1)S(1)} %pad_maximum_fusion.1.refs_1_, bf16[4,64,256]{2,1,0:T(8,128)(2,1)S(1)} %collective-permute-done.8.refs_2_), custom_call_target="tpu_custom_call" | custom-call | flops 6400000000 | bytes 4000000 | tf_op jit(solution)/shard_map/pallas_call | solution.py:124
  27.2 3.8 %collective-permute-start.9 = (bf16[8,64,256]{2,1,0:T(8,128)(2,1)S(1)}, bf16[8,64,256]{2,1,0:T(8,128)(2,1)S(1)}, u32[]{:S(2)}, u32[]{:S(2)}) collective-permute-start(bf16[8,64,256]{2,1,0:T(8,128)(2,1)S(1)} %pad_maximum_fusion), channel_id=1, source_target_pairs={{0,34},{1,35},{2,32},{3,33},{4,38},{5,39},{6,36},{7,37},{8,42},{9,... | collective-permute-start | bytes 786440 | tf_op jit(solution)/shard_map/ppermute | solution.py:146
  31.0 9.6 %shard_map.69 = (f32[12,56,256]{2,1,0:T(8,128)S(1)}, f32[4,8,256]{2,1,0:T(8,128)S(1)}) custom-call(bf16[4,64,256]{2,1,0:T(8,128)(2,1)S(1)} %collective-permute-done.7.refs_0_.refs_1_, bf16[4,64,256]{2,1,0:T(8,128)(2,1)S(1)} %pad_maximum_fusion.1.refs_1_, bf16[4,64,256]{2,1,0:T(8,128)(2,1)S(1)} %collective-permute-done.8.refs_2_, ...), custom_call_target="tpu_custom_call" | custom-call | flops 9600000000 | bytes 4000000 | tf_op jit(solution)/shard_map/pallas_call | solution.py:124
  40.6 2.2 %collective-permute-done.9.refs_2_.refs_3_.refs_1_.refs_0_ = bf16[8,64,256]{2,1,0:T(8,128)(2,1)S(1)} collective-permute-done((bf16[8,64,256]{2,1,0:T(8,128)(2,1)S(1)}, bf16[8,64,256]{2,1,0:T(8,128)(2,1)S(1)}, u32[]{:S(2)}, u32[]{:S(2)}) %collective-permute-start.9) | collective-permute-done | bytes 262176 | tf_op jit(solution)/shard_map/ppermute | solution.py:146
  42.8 11.7 %shard_map.70 = (f32[4,56,256]{2,1,0:T(8,128)S(1)}, f32[4,8,256]{2,1,0:T(8,128)S(1)}, f32[4,8,256]{2,1,0:T(8,128)S(1)}, f32[4,8,256]{2,1,0:T(8,128)S(1)}, f32[4,8,256]{2,1,0:T(8,128)S(1)}) custom-call(bf16[4,64,256]{2,1,0:T(8,128)(2,1)S(1)} %pad_maximum_fusion.2.refs_0_, bf16[4,64,256]{2,1,0:T(8,128)(2,1)S(1)} %collective-permute-done.7.refs_0_.refs_1_, ...), custom_call_target="tpu_custom_call" | custom-call | flops 12800000000 | bytes 4000000 | tf_op jit(solution)/shard_map/pallas_call | solution.py:124
  54.8 9.0 %shard_map.71 = (f32[4,56,256]{2,1,0:T(8,128)S(1)}, f32[4,8,256]{2,1,0:T(8,128)S(1)}, f32[4,8,256]{2,1,0:T(8,128)S(1)}, f32[4,8,256]{2,1,0:T(8,128)S(1)}) custom-call(bf16[4,64,256]{2,1,0:T(8,128)(2,1)S(1)} %pad_maximum_fusion.2.refs_0_, bf16[8,64,256]{2,1,0:T(8,128)(2,1)S(1)} %collective-permute-done.9.refs_2_.refs_3_.refs_1_.refs_0_, ...), custom_call_target="tpu_custom_call" | custom-call | flops 9600000000 | bytes 4000000 | tf_op jit(solution)/shard_map/pallas_call | solution.py:124
  63.8 2.6 %collective-permute-start.14 = (f32[4,56,256]{2,1,0:T(8,128)S(1)}, f32[4,56,256]{2,1,0:T(8,128)S(1)}, u32[]{:S(2)}, u32[]{:S(2)}) collective-permute-start(f32[4,56,256]{2,1,0:T(8,128)S(1)} %add.36), channel_id=1, source_target_pairs={{0,1},{1,0},{2,3},{3,2},{4,5},{5,4},{6,7},{7,6},{8,9},{9,8},{10,11... | collective-permute-start | bytes 688136 | tf_op jit(solution)/shard_map/ppermute | solution.py:146
  66.4 6.0 %shard_map.72 = (f32[4,56,256]{2,1,0:T(8,128)S(1)}, f32[4,8,256]{2,1,0:T(8,128)S(1)}, f32[4,8,256]{2,1,0:T(8,128)S(1)}) custom-call(bf16[8,64,256]{2,1,0:T(8,128)(2,1)S(1)} %collective-permute-done.9.refs_2_.refs_3_.refs_1_.refs_0_, bf16[8,64,256]{2,1,0:T(8,128)(2,1)S(1)} %collective-permute-done.9.refs_2_.refs_3_.refs_1_.refs_0_, ...), custom_call_target="tpu_custom_call" | custom-call | flops 6400000000 | bytes 4000000 | tf_op jit(solution)/shard_map/pallas_call | solution.py:124
  72.5 3.3 %shard_map.73 = (f32[4,56,256]{2,1,0:T(8,128)S(1)}, f32[4,8,256]{2,1,0:T(8,128)S(1)}) custom-call(bf16[8,64,256]{2,1,0:T(8,128)(2,1)S(1)} %collective-permute-done.9.refs_2_.refs_3_.refs_1_.refs_0_, bf16[4,64,256]{2,1,0:T(8,128)(2,1)S(1)} %pad_maximum_fusion.1.refs_1_, f32[8,56,256]{2,1,0:T(8,128)S(1)} %get-tuple-element.60.refs_3_.refs_2_, ...), custom_call_target="tpu_custom_call" | custom-call | flops 3200000000 | bytes 4000000 | tf_op jit(solution)/shard_map/pallas_call | solution.py:124
  75.8 1.0 %collective-permute-start.12 = (f32[8,8,256]{2,1,0:T(8,128)S(1)}, f32[8,8,256]{2,1,0:T(8,128)S(1)}, u32[]{:S(2)}, u32[]{:S(2)}) collective-permute-start(f32[8,8,256]{2,1,0:T(8,128)S(1)} %pad_maximum_fusion.3), channel_id=1, source_target_pairs={{0,2},{1,3},{2,0},{3,1},{4,6},{5,7},{6,4},{7,5},{8,10},{9,11},{10,... | collective-permute-start | bytes 196616 | tf_op jit(solution)/shard_map/ppermute | solution.py:146
  76.9 3.3 %shard_map.74 = (f32[4,56,256]{2,1,0:T(8,128)S(1)}, f32[4,8,256]{2,1,0:T(8,128)S(1)}) custom-call(bf16[8,64,256]{2,1,0:T(8,128)(2,1)S(1)} %collective-permute-done.9.refs_2_.refs_3_.refs_1_.refs_0_, bf16[4,64,256]{2,1,0:T(8,128)(2,1)S(1)} %pad_maximum_fusion.1.refs_1_, f32[4,56,256]{2,1,0:T(8,128)S(1)} %get-tuple-element.64.refs_2_, ...), custom_call_target="tpu_custom_call" | custom-call | flops 3200000000 | bytes 4000000 | tf_op jit(solution)/shard_map/pallas_call | solution.py:124
  80.2 1.8 %collective-permute-done.12 = f32[8,8,256]{2,1,0:T(8,128)S(1)} collective-permute-done((f32[8,8,256]{2,1,0:T(8,128)S(1)}, f32[8,8,256]{2,1,0:T(8,128)S(1)}, u32[]{:S(2)}, u32[]{:S(2)}) %collective-permute-start.12) | collective-permute-done | bytes 65568 | tf_op jit(solution)/shard_map/ppermute | solution.py:146
  82.0 1.8 %collective-permute-start.18 = (f32[4,8,256]{2,1,0:T(8,128)S(1)}, f32[4,8,256]{2,1,0:T(8,128)S(1)}, u32[]{:S(2)}, u32[]{:S(2)}) collective-permute-start(f32[4,8,256]{2,1,0:T(8,128)S(1)} %slice_add_fusion), channel_id=1, source_target_pairs={{0,34},{1,35},{2,32},{3,33},{4,38},{5,39},{6,36},{7,37},{8,42},{9,... | collective-permute-start | bytes 98312 | tf_op jit(solution)/shard_map/ppermute | solution.py:146
  83.9 1.2 %collective-permute-start.17 = (bf16[56,256]{1,0:T(8,128)(2,1)S(1)}, bf16[56,256]{1,0:T(8,128)(2,1)S(1)}, u32[]{:S(2)}, u32[]{:S(2)}) collective-permute-start(bf16[56,256]{1,0:T(8,128)(2,1)S(1)} %get-tuple-element.87), channel_id=1, source_target_pairs={{0,128},{1,129},{2,130},{3,131},{4,132},{5,133},{6,134},{7,135},{8... | collective-permute-start | bytes 86024 | tf_op jit(solution)/shard_map/ppermute | solution.py:146
  85.7 3.0 %collective-permute-start.15 = (bf16[56,256]{1,0:T(8,128)(2,1)S(1)}, bf16[56,256]{1,0:T(8,128)(2,1)S(1)}, u32[]{:S(2)}, u32[]{:S(2)}) collective-permute-start(bf16[56,256]{1,0:T(8,128)(2,1)S(1)} %get-tuple-element.89), channel_id=1, source_target_pairs={{0,64},{1,65},{2,66},{3,67},{4,68},{5,69},{6,70},{7,71},{8,72},{9,... | collective-permute-start | bytes 86024 | tf_op jit(solution)/shard_map/ppermute | solution.py:146
  88.8 1.6 %collective-permute-start.21 = (f32[8,256]{1,0:T(8,128)S(1)}, f32[8,256]{1,0:T(8,128)S(1)}, u32[]{:S(2)}, u32[]{:S(2)}) collective-permute-start(f32[8,256]{1,0:T(8,128)S(1)} %get-tuple-element.90), channel_id=1, source_target_pairs={{0,8},{1,9},{2,10},{3,11},{4,12},{5,13},{6,14},{7,15},{8,0},{9,1},... | collective-permute-start | bytes 24584 | tf_op jit(solution)/shard_map/ppermute | solution.py:146
  90.3 1.2 %collective-permute-start.20 = (f32[8,256]{1,0:T(8,128)S(1)}, f32[8,256]{1,0:T(8,128)S(1)}, u32[]{:S(2)}, u32[]{:S(2)}) collective-permute-start(f32[8,256]{1,0:T(8,128)S(1)} %get-tuple-element.91), channel_id=1, source_target_pairs={{0,12},{1,13},{2,14},{3,15},{4,8},{5,9},{6,10},{7,11},{8,4},{9,5},... | collective-permute-start | bytes 24584 | tf_op jit(solution)/shard_map/ppermute | solution.py:146
  91.5 0.8 collective-permute-start.19
  92.4 1.6 %collective-permute-done.21 = f32[8,256]{1,0:T(8,128)S(1)} collective-permute-done((f32[8,256]{1,0:T(8,128)S(1)}, f32[8,256]{1,0:T(8,128)S(1)}, u32[]{:S(2)}, u32[]{:S(2)}) %collective-permute-start.21) | collective-permute-done | bytes 8224 | tf_op jit(solution)/shard_map/ppermute | solution.py:146
  94.0 1.2 %collective-permute-done.20 = f32[8,256]{1,0:T(8,128)S(1)} collective-permute-done((f32[8,256]{1,0:T(8,128)S(1)}, f32[8,256]{1,0:T(8,128)S(1)}, u32[]{:S(2)}, u32[]{:S(2)}) %collective-permute-start.20) | collective-permute-done | bytes 8224 | tf_op jit(solution)/shard_map/ppermute | solution.py:146
  95.8 0.6 slice.60
  (37 shorter events, 2.6 us)
Async XLA Ops:
  2.1 8.9 %collective-permute-start.2 = (bf16[1,64,256]{2,1,0:T(8,128)(2,1)}, bf16[1,64,256]{2,1,0:T(8,128)(2,1)S(1)}, u32[]{:S(2)}, u32[]{:S(2)}) collective-permute-start(bf16[1,64,256]{2,1,0:T(8,128)(2,1)} %get-tuple-element.44), channel_id=1, source_target_pairs={{0,128},{1,129},{2,130},{3,131},{4,132},{5,133},{6,134},{7,135},{8... | collective-permute-start | bytes 98312 | tf_op jit(solution)/shard_map/ppermute | solution.py:146
  4.4 6.6 %collective-permute-start.1 = (bf16[1,64,256]{2,1,0:T(8,128)(2,1)}, bf16[1,64,256]{2,1,0:T(8,128)(2,1)S(1)}, u32[]{:S(2)}, u32[]{:S(2)}) collective-permute-start(bf16[1,64,256]{2,1,0:T(8,128)(2,1)} %get-tuple-element.44), channel_id=1, source_target_pairs={{0,192},{1,193},{2,194},{3,195},{4,196},{5,197},{6,198},{7,199},{8... | collective-permute-start | bytes 98312 | tf_op jit(solution)/shard_map/ppermute | solution.py:146
  5.7 5.2 %collective-permute-start = (bf16[1,64,256]{2,1,0:T(8,128)(2,1)}, bf16[1,64,256]{2,1,0:T(8,128)(2,1)S(1)}, u32[]{:S(2)}, u32[]{:S(2)}) collective-permute-start(bf16[1,64,256]{2,1,0:T(8,128)(2,1)} %get-tuple-element.44), channel_id=1, source_target_pairs={{0,64},{1,65},{2,66},{3,67},{4,68},{5,69},{6,70},{7,71},{8,72},{9,... | collective-permute-start | bytes 98312 | tf_op jit(solution)/shard_map/ppermute | solution.py:146
  6.8 8.4 %copy-start = (bf16[1,64,256]{2,1,0:T(8,128)(2,1)S(1)}, bf16[1,64,256]{2,1,0:T(8,128)(2,1)}, u32[]{:S(2)}) copy-start(bf16[1,64,256]{2,1,0:T(8,128)(2,1)} %get-tuple-element.45) | copy-start | bytes 98308
  6.8 5.6 %collective-permute-start.5 = (bf16[1,64,256]{2,1,0:T(8,128)(2,1)}, bf16[1,64,256]{2,1,0:T(8,128)(2,1)S(1)}, u32[]{:S(2)}, u32[]{:S(2)}) collective-permute-start(bf16[1,64,256]{2,1,0:T(8,128)(2,1)} %get-tuple-element.45), channel_id=1, source_target_pairs={{0,8},{1,9},{2,10},{3,11},{4,12},{5,13},{6,14},{7,15},{8,0},{9,1},... | collective-permute-start | bytes 98312 | tf_op jit(solution)/shard_map/ppermute | solution.py:146
  9.8 5.3 %collective-permute-start.4 = (bf16[1,64,256]{2,1,0:T(8,128)(2,1)}, bf16[1,64,256]{2,1,0:T(8,128)(2,1)S(1)}, u32[]{:S(2)}, u32[]{:S(2)}) collective-permute-start(bf16[1,64,256]{2,1,0:T(8,128)(2,1)} %get-tuple-element.45), channel_id=1, source_target_pairs={{0,12},{1,13},{2,14},{3,15},{4,8},{5,9},{6,10},{7,11},{8,4},{9,5},... | collective-permute-start | bytes 98312 | tf_op jit(solution)/shard_map/ppermute | solution.py:146
  10.9 4.2 %collective-permute-start.3 = (bf16[1,64,256]{2,1,0:T(8,128)(2,1)}, bf16[1,64,256]{2,1,0:T(8,128)(2,1)S(1)}, u32[]{:S(2)}, u32[]{:S(2)}) collective-permute-start(bf16[1,64,256]{2,1,0:T(8,128)(2,1)} %get-tuple-element.45), channel_id=1, source_target_pairs={{0,4},{1,5},{2,6},{3,7},{4,0},{5,1},{6,2},{7,3},{8,12},{9,13},{10,... | collective-permute-start | bytes 98312 | tf_op jit(solution)/shard_map/ppermute | solution.py:146
  15.2 5.4 %collective-permute-start.8 = (bf16[4,64,256]{2,1,0:T(8,128)(2,1)S(1)}, bf16[4,64,256]{2,1,0:T(8,128)(2,1)S(1)}, u32[]{:S(2)}, u32[]{:S(2)}) collective-permute-start(bf16[4,64,256]{2,1,0:T(8,128)(2,1)S(1)} %pad_maximum_fusion.1.refs_1_), channel_id=1, source_target_pairs={{0,16},{1,17},{2,18},{3,19},{4,20},{5,21},{6,22},{7,23},{8,24},{9,... | collective-permute-start | bytes 393224 | tf_op jit(solution)/shard_map/ppermute | solution.py:146
  15.3 11.9 %collective-permute-start.6 = (bf16[4,64,256]{2,1,0:T(8,128)(2,1)S(1)}, bf16[4,64,256]{2,1,0:T(8,128)(2,1)S(1)}, u32[]{:S(2)}, u32[]{:S(2)}) collective-permute-start(bf16[4,64,256]{2,1,0:T(8,128)(2,1)S(1)} %pad_maximum_fusion.1.refs_1_), channel_id=1, source_target_pairs={{0,1},{1,0},{2,3},{3,2},{4,5},{5,4},{6,7},{7,6},{8,9},{9,8},{10,11... | collective-permute-start | bytes 393224 | tf_op jit(solution)/shard_map/ppermute | solution.py:146
  17.3 9.9 %collective-permute-start.7 = (bf16[4,64,256]{2,1,0:T(8,128)(2,1)S(1)}, bf16[4,64,256]{2,1,0:T(8,128)(2,1)S(1)}, u32[]{:S(2)}, u32[]{:S(2)}) collective-permute-start(bf16[4,64,256]{2,1,0:T(8,128)(2,1)S(1)} %pad_maximum_fusion.2.refs_0_), channel_id=1, source_target_pairs={{0,2},{1,3},{2,0},{3,1},{4,6},{5,7},{6,4},{7,5},{8,10},{9,11},{10,... | collective-permute-start | bytes 393224 | tf_op jit(solution)/shard_map/ppermute | solution.py:146
  27.2 13.4 %collective-permute-start.10 = (bf16[4,64,256]{2,1,0:T(8,128)(2,1)S(1)}, bf16[4,64,256]{2,1,0:T(8,128)(2,1)S(1)}, u32[]{:S(2)}, u32[]{:S(2)}) collective-permute-start(bf16[4,64,256]{2,1,0:T(8,128)(2,1)S(1)} %collective-permute-done.6.refs_3_), channel_id=1, source_target_pairs={{0,16},{1,17},{2,18},{3,19},{4,20},{5,21},{6,22},{7,23},{8,24},{9,... | collective-permute-start | bytes 393224 | tf_op jit(solution)/shard_map/ppermute | solution.py:146
  27.2 15.6 %collective-permute-start.9 = (bf16[8,64,256]{2,1,0:T(8,128)(2,1)S(1)}, bf16[8,64,256]{2,1,0:T(8,128)(2,1)S(1)}, u32[]{:S(2)}, u32[]{:S(2)}) collective-permute-start(bf16[8,64,256]{2,1,0:T(8,128)(2,1)S(1)} %pad_maximum_fusion), channel_id=1, source_target_pairs={{0,34},{1,35},{2,32},{3,33},{4,38},{5,39},{6,36},{7,37},{8,42},{9,... | collective-permute-start | bytes 786440 | tf_op jit(solution)/shard_map/ppermute | solution.py:146
  54.5 9.3 %collective-permute-start.11 = (f32[4,56,256]{2,1,0:T(8,128)S(1)}, f32[4,56,256]{2,1,0:T(8,128)S(1)}, u32[]{:S(2)}, u32[]{:S(2)}) collective-permute-start(f32[4,56,256]{2,1,0:T(8,128)S(1)} %get-tuple-element.58), channel_id=1, source_target_pairs={{0,16},{1,17},{2,18},{3,19},{4,20},{5,21},{6,22},{7,23},{8,24},{9,... | collective-permute-start | bytes 688136 | tf_op jit(solution)/shard_map/ppermute | solution.py:146
  63.8 18.2 %collective-permute-start.14 = (f32[4,56,256]{2,1,0:T(8,128)S(1)}, f32[4,56,256]{2,1,0:T(8,128)S(1)}, u32[]{:S(2)}, u32[]{:S(2)}) collective-permute-start(f32[4,56,256]{2,1,0:T(8,128)S(1)} %add.36), channel_id=1, source_target_pairs={{0,1},{1,0},{2,3},{3,2},{4,5},{5,4},{6,7},{7,6},{8,9},{9,8},{10,11... | collective-permute-start | bytes 688136 | tf_op jit(solution)/shard_map/ppermute | solution.py:146
  75.8 6.2 %collective-permute-start.12 = (f32[8,8,256]{2,1,0:T(8,128)S(1)}, f32[8,8,256]{2,1,0:T(8,128)S(1)}, u32[]{:S(2)}, u32[]{:S(2)}) collective-permute-start(f32[8,8,256]{2,1,0:T(8,128)S(1)} %pad_maximum_fusion.3), channel_id=1, source_target_pairs={{0,2},{1,3},{2,0},{3,1},{4,6},{5,7},{6,4},{7,5},{8,10},{9,11},{10,... | collective-permute-start | bytes 196616 | tf_op jit(solution)/shard_map/ppermute | solution.py:146
  76.8 5.2 %collective-permute-start.13 = (f32[4,56,256]{2,1,0:T(8,128)S(1)}, f32[4,56,256]{2,1,0:T(8,128)S(1)}, u32[]{:S(2)}, u32[]{:S(2)}) collective-permute-start(f32[4,56,256]{2,1,0:T(8,128)S(1)} %get-tuple-element.70), channel_id=1, source_target_pairs={{0,16},{1,17},{2,18},{3,19},{4,20},{5,21},{6,22},{7,23},{8,24},{9,... | collective-permute-start | bytes 688136 | tf_op jit(solution)/shard_map/ppermute | solution.py:146
  82.0 6.7 %collective-permute-start.18 = (f32[4,8,256]{2,1,0:T(8,128)S(1)}, f32[4,8,256]{2,1,0:T(8,128)S(1)}, u32[]{:S(2)}, u32[]{:S(2)}) collective-permute-start(f32[4,8,256]{2,1,0:T(8,128)S(1)} %slice_add_fusion), channel_id=1, source_target_pairs={{0,34},{1,35},{2,32},{3,33},{4,38},{5,39},{6,36},{7,37},{8,42},{9,... | collective-permute-start | bytes 98312 | tf_op jit(solution)/shard_map/ppermute | solution.py:146
  83.9 7.5 %collective-permute-start.17 = (bf16[56,256]{1,0:T(8,128)(2,1)S(1)}, bf16[56,256]{1,0:T(8,128)(2,1)S(1)}, u32[]{:S(2)}, u32[]{:S(2)}) collective-permute-start(bf16[56,256]{1,0:T(8,128)(2,1)S(1)} %get-tuple-element.87), channel_id=1, source_target_pairs={{0,128},{1,129},{2,130},{3,131},{4,132},{5,133},{6,134},{7,135},{8... | collective-permute-start | bytes 86024 | tf_op jit(solution)/shard_map/ppermute | solution.py:146
  85.1 7.2 %collective-permute-start.16 = (bf16[56,256]{1,0:T(8,128)(2,1)S(1)}, bf16[56,256]{1,0:T(8,128)(2,1)S(1)}, u32[]{:S(2)}, u32[]{:S(2)}) collective-permute-start(bf16[56,256]{1,0:T(8,128)(2,1)S(1)} %get-tuple-element.88), channel_id=1, source_target_pairs={{0,192},{1,193},{2,194},{3,195},{4,196},{5,197},{6,198},{7,199},{8... | collective-permute-start | bytes 86024 | tf_op jit(solution)/shard_map/ppermute | solution.py:146
  85.7 6.6 %collective-permute-start.15 = (bf16[56,256]{1,0:T(8,128)(2,1)S(1)}, bf16[56,256]{1,0:T(8,128)(2,1)S(1)}, u32[]{:S(2)}, u32[]{:S(2)}) collective-permute-start(bf16[56,256]{1,0:T(8,128)(2,1)S(1)} %get-tuple-element.89), channel_id=1, source_target_pairs={{0,64},{1,65},{2,66},{3,67},{4,68},{5,69},{6,70},{7,71},{8,72},{9,... | collective-permute-start | bytes 86024 | tf_op jit(solution)/shard_map/ppermute | solution.py:146
  88.8 5.2 %collective-permute-start.21 = (f32[8,256]{1,0:T(8,128)S(1)}, f32[8,256]{1,0:T(8,128)S(1)}, u32[]{:S(2)}, u32[]{:S(2)}) collective-permute-start(f32[8,256]{1,0:T(8,128)S(1)} %get-tuple-element.90), channel_id=1, source_target_pairs={{0,8},{1,9},{2,10},{3,11},{4,12},{5,13},{6,14},{7,15},{8,0},{9,1},... | collective-permute-start | bytes 24584 | tf_op jit(solution)/shard_map/ppermute | solution.py:146
  90.3 4.9 %collective-permute-start.20 = (f32[8,256]{1,0:T(8,128)S(1)}, f32[8,256]{1,0:T(8,128)S(1)}, u32[]{:S(2)}, u32[]{:S(2)}) collective-permute-start(f32[8,256]{1,0:T(8,128)S(1)} %get-tuple-element.91), channel_id=1, source_target_pairs={{0,12},{1,13},{2,14},{3,15},{4,8},{5,9},{6,10},{7,11},{8,4},{9,5},... | collective-permute-start | bytes 24584 | tf_op jit(solution)/shard_map/ppermute | solution.py:146
  91.5 3.7 %collective-permute-start.19 = (f32[8,256]{1,0:T(8,128)S(1)}, f32[8,256]{1,0:T(8,128)S(1)}, u32[]{:S(2)}, u32[]{:S(2)}) collective-permute-start(f32[8,256]{1,0:T(8,128)S(1)} %get-tuple-element.92), channel_id=1, source_target_pairs={{0,4},{1,5},{2,6},{3,7},{4,0},{5,1},{6,2},{7,3},{8,12},{9,13},{10,... | collective-permute-start | bytes 24584 | tf_op jit(solution)/shard_map/ppermute | solution.py:146

commit v2 on v1

--- a/solution.py
+++ b/solution.py
@@ -166,10 +166,10 @@
 
 def shards(vol_coords, vol_cotangent, ctl_coords, ctl_weights):
     v, c = pack(vol_coords, vol_cotangent, ctl_coords, ctl_weights)
-    cp, va = tie(gather(c, Y_MASKS), gather(v, X_MASKS))
+    va, cp = tie(gather(v, X_MASKS), gather(c, Y_MASKS))
+    vb = swap(va, Z_TWO)
     cq = swap(cp, CORE)
     cr = swap(cp, Z_ONE)
-    vb = swap(va, Z_TWO)
     a = (va, 0)
     pq, sum_a = pair_sums([a], [(cp, 0), (cq, 0)], [None])
     cr, vb, pq = tie(cr, vb, pq)

time: 97.8 us -> 98.3 us (level)
  transfers between devices with their start and end apart: 22 -> 22, of which waited for: 7 -> 8; matrix products, arithmetic and copies ran while one was open for 1% -> 1% of each run, Pallas kernels for 39% -> 39%
where the time goes in v2:
time: 98.3 us; the launch traced here: 97 us
  Pallas kernels  50.7 us (52%)
  starting transfers between devices  33.1 us (34%)
  waiting for transfers between devices  9.57 us (10%)
  other arithmetic  1.53 us (2%)
  local copies, waits for them, and re-layouts  1.24 us (1%)
    pallas_call x7, Pallas kernels, pair_sums(): pl.pallas_call(body, out_shape=[jax.ShapeDtypeStruct((c_count, 56, BLOCK)...  49.3 us
    ppermute x22, starting transfers between devices, swap(): lax.ppermute(value, ('vol', 'ctl'), [(i, i ^ mask) for i in range(256)])  33.1 us
    ppermute x22, waiting for transfers between devices, swap(): lax.ppermute(value, ('vol', 'ctl'), [(i, i ^ mask) for i in range(256)])  9.57 us
  transfers between devices with their start and end apart: 22, of which 8 were waited for; matrix products, arithmetic and copies ran while one was open for 1% of the time, Pallas kernels for 39%

profile of v2, /device:TPU:8, one launch (start us, length us, event | category | flops | bytes accessed | tf_op | source)
XLA Modules:
  0.0 97.0 jit_solution(12374327561664732875)
XLA Ops:
  0.6 1.4 %shard_map.67 = (bf16[1,64,256]{2,1,0:T(8,128)(2,1)}, bf16[1,64,256]{2,1,0:T(8,128)(2,1)}) custom-call(bf16[3,256]{1,0:T(4,128)(2,1)} %vx_ref.1, bf16[48,256]{1,0:T(8,128)(2,1)} %vc_ref.1, bf16[3,256]{1,0:T(4,128)(2,1)} %cx_ref.1, bf16[48,256]{1,0:T(8,128)(2,1)} %cw_ref.1), custom_call_target="tpu_custom_call" | custom-call | tf_op jit(solution)/shard_map/pallas_call | solution.py:41
  2.1 3.0 %collective-permute-start.2 = (bf16[1,64,256]{2,1,0:T(8,128)(2,1)}, bf16[1,64,256]{2,1,0:T(8,128)(2,1)S(1)}, u32[]{:S(2)}, u32[]{:S(2)}) collective-permute-start(bf16[1,64,256]{2,1,0:T(8,128)(2,1)} %get-tuple-element.44), channel_id=1, source_target_pairs={{0,8},{1,9},{2,10},{3,11},{4,12},{5,13},{6,14},{7,15},{8,0},{9,1},... | collective-permute-start | bytes 98312 | tf_op jit(solution)/shard_map/ppermute | solution.py:146
  5.1 1.1 %collective-permute-start.1 = (bf16[1,64,256]{2,1,0:T(8,128)(2,1)}, bf16[1,64,256]{2,1,0:T(8,128)(2,1)S(1)}, u32[]{:S(2)}, u32[]{:S(2)}) collective-permute-start(bf16[1,64,256]{2,1,0:T(8,128)(2,1)} %get-tuple-element.44), channel_id=1, source_target_pairs={{0,12},{1,13},{2,14},{3,15},{4,8},{5,9},{6,10},{7,11},{8,4},{9,5},... | collective-permute-start | bytes 98312 | tf_op jit(solution)/shard_map/ppermute | solution.py:146
  6.2 2.3 %collective-permute-start.5 = (bf16[1,64,256]{2,1,0:T(8,128)(2,1)}, bf16[1,64,256]{2,1,0:T(8,128)(2,1)S(1)}, u32[]{:S(2)}, u32[]{:S(2)}) collective-permute-start(bf16[1,64,256]{2,1,0:T(8,128)(2,1)} %get-tuple-element.45), channel_id=1, source_target_pairs={{0,128},{1,129},{2,130},{3,131},{4,132},{5,133},{6,134},{7,135},{8... | collective-permute-start | bytes 98312 | tf_op jit(solution)/shard_map/ppermute | solution.py:146
  8.5 0.7 collective-permute-start.4
  9.2 1.7 %collective-permute-start.3 = (bf16[1,64,256]{2,1,0:T(8,128)(2,1)}, bf16[1,64,256]{2,1,0:T(8,128)(2,1)S(1)}, u32[]{:S(2)}, u32[]{:S(2)}) collective-permute-start(bf16[1,64,256]{2,1,0:T(8,128)(2,1)} %get-tuple-element.45), channel_id=1, source_target_pairs={{0,64},{1,65},{2,66},{3,67},{4,68},{5,69},{6,70},{7,71},{8,72},{9,... | collective-permute-start | bytes 98312 | tf_op jit(solution)/shard_map/ppermute | solution.py:146
  11.0 0.8 pad_maximum_fusion.1.refs_0_
  12.0 0.7 collective-permute-done.4
  12.7 0.7 collective-permute-done.3
  13.5 1.7 %collective-permute-start.6 = (bf16[4,64,256]{2,1,0:T(8,128)(2,1)S(1)}, bf16[4,64,256]{2,1,0:T(8,128)(2,1)S(1)}, u32[]{:S(2)}, u32[]{:S(2)}) collective-permute-start(bf16[4,64,256]{2,1,0:T(8,128)(2,1)S(1)} %pad_maximum_fusion.2.refs_1_), channel_id=1, source_target_pairs={{0,1},{1,0},{2,3},{3,2},{4,5},{5,4},{6,7},{7,6},{8,9},{9,8},{10,11... | collective-permute-start | bytes 393224 | tf_op jit(solution)/shard_map/ppermute | solution.py:146
  15.2 3.3 %collective-permute-start.7 = (bf16[4,64,256]{2,1,0:T(8,128)(2,1)S(1)}, bf16[4,64,256]{2,1,0:T(8,128)(2,1)S(1)}, u32[]{:S(2)}, u32[]{:S(2)}) collective-permute-start(bf16[4,64,256]{2,1,0:T(8,128)(2,1)S(1)} %pad_maximum_fusion.1.refs_0_), channel_id=1, source_target_pairs={{0,2},{1,3},{2,0},{3,1},{4,6},{5,7},{6,4},{7,5},{8,10},{9,11},{10,... | collective-permute-start | bytes 393224 | tf_op jit(solution)/shard_map/ppermute | solution.py:146
  18.5 6.4 %shard_map.68 = (f32[8,56,256]{2,1,0:T(8,128)S(1)}, f32[4,8,256]{2,1,0:T(8,128)S(1)}) custom-call(bf16[4,64,256]{2,1,0:T(8,128)(2,1)S(1)} %pad_maximum_fusion.1.refs_0_, bf16[4,64,256]{2,1,0:T(8,128)(2,1)S(1)} %pad_maximum_fusion.2.refs_1_, bf16[4,64,256]{2,1,0:T(8,128)(2,1)S(1)} %collective-permute-done.8.refs_2_), custom_call_target="tpu_custom_call" | custom-call | flops 6400000000 | bytes 4000000 | tf_op jit(solution)/shard_map/pallas_call | solution.py:124
  25.1 3.8 %collective-permute-start.9 = (bf16[8,64,256]{2,1,0:T(8,128)(2,1)S(1)}, bf16[8,64,256]{2,1,0:T(8,128)(2,1)S(1)}, u32[]{:S(2)}, u32[]{:S(2)}) collective-permute-start(bf16[8,64,256]{2,1,0:T(8,128)(2,1)S(1)} %pad_maximum_fusion), channel_id=1, source_target_pairs={{0,34},{1,35},{2,32},{3,33},{4,38},{5,39},{6,36},{7,37},{8,42},{9,... | collective-permute-start | bytes 786440 | tf_op jit(solution)/shard_map/ppermute | solution.py:146
  28.9 9.6 %shard_map.69 = (f32[12,56,256]{2,1,0:T(8,128)S(1)}, f32[4,8,256]{2,1,0:T(8,128)S(1)}) custom-call(bf16[4,64,256]{2,1,0:T(8,128)(2,1)S(1)} %collective-permute-done.7.refs_0_.refs_1_, bf16[4,64,256]{2,1,0:T(8,128)(2,1)S(1)} %pad_maximum_fusion.2.refs_1_, bf16[4,64,256]{2,1,0:T(8,128)(2,1)S(1)} %collective-permute-done.8.refs_2_, ...), custom_call_target="tpu_custom_call" | custom-call | flops 9600000000 | bytes 4000000 | tf_op jit(solution)/shard_map/pallas_call | solution.py:124
  38.5 2.3 %collective-permute-done.9.refs_2_.refs_3_.refs_1_.refs_0_ = bf16[8,64,256]{2,1,0:T(8,128)(2,1)S(1)} collective-permute-done((bf16[8,64,256]{2,1,0:T(8,128)(2,1)S(1)}, bf16[8,64,256]{2,1,0:T(8,128)(2,1)S(1)}, u32[]{:S(2)}, u32[]{:S(2)}) %collective-permute-start.9) | collective-permute-done | bytes 262176 | tf_op jit(solution)/shard_map/ppermute | solution.py:146
  40.8 11.7 %shard_map.70 = (f32[4,56,256]{2,1,0:T(8,128)S(1)}, f32[4,8,256]{2,1,0:T(8,128)S(1)}, f32[4,8,256]{2,1,0:T(8,128)S(1)}, f32[4,8,256]{2,1,0:T(8,128)S(1)}, f32[4,8,256]{2,1,0:T(8,128)S(1)}) custom-call(bf16[4,64,256]{2,1,0:T(8,128)(2,1)S(1)} %pad_maximum_fusion.1.refs_0_, bf16[4,64,256]{2,1,0:T(8,128)(2,1)S(1)} %collective-permute-done.7.refs_0_.refs_1_, ...), custom_call_target="tpu_custom_call" | custom-call | flops 12800000000 | bytes 4000000 | tf_op jit(solution)/shard_map/pallas_call | solution.py:124
  52.7 9.0 %shard_map.71 = (f32[4,56,256]{2,1,0:T(8,128)S(1)}, f32[4,8,256]{2,1,0:T(8,128)S(1)}, f32[4,8,256]{2,1,0:T(8,128)S(1)}, f32[4,8,256]{2,1,0:T(8,128)S(1)}) custom-call(bf16[4,64,256]{2,1,0:T(8,128)(2,1)S(1)} %pad_maximum_fusion.1.refs_0_, bf16[8,64,256]{2,1,0:T(8,128)(2,1)S(1)} %collective-permute-done.9.refs_2_.refs_3_.refs_1_.refs_0_, ...), custom_call_target="tpu_custom_call" | custom-call | flops 9600000000 | bytes 4000000 | tf_op jit(solution)/shard_map/pallas_call | solution.py:124
  61.8 2.6 %collective-permute-start.14 = (f32[4,56,256]{2,1,0:T(8,128)S(1)}, f32[4,56,256]{2,1,0:T(8,128)S(1)}, u32[]{:S(2)}, u32[]{:S(2)}) collective-permute-start(f32[4,56,256]{2,1,0:T(8,128)S(1)} %add.36), channel_id=1, source_target_pairs={{0,1},{1,0},{2,3},{3,2},{4,5},{5,4},{6,7},{7,6},{8,9},{9,8},{10,11... | collective-permute-start | bytes 688136 | tf_op jit(solution)/shard_map/ppermute | solution.py:146
  64.3 6.0 %shard_map.72 = (f32[4,56,256]{2,1,0:T(8,128)S(1)}, f32[4,8,256]{2,1,0:T(8,128)S(1)}, f32[4,8,256]{2,1,0:T(8,128)S(1)}) custom-call(bf16[8,64,256]{2,1,0:T(8,128)(2,1)S(1)} %collective-permute-done.9.refs_2_.refs_3_.refs_1_.refs_0_, bf16[8,64,256]{2,1,0:T(8,128)(2,1)S(1)} %collective-permute-done.9.refs_2_.refs_3_.refs_1_.refs_0_, ...), custom_call_target="tpu_custom_call" | custom-call | flops 6400000000 | bytes 4000000 | tf_op jit(solution)/shard_map/pallas_call | solution.py:124
  70.4 3.3 %shard_map.73 = (f32[4,56,256]{2,1,0:T(8,128)S(1)}, f32[4,8,256]{2,1,0:T(8,128)S(1)}) custom-call(bf16[8,64,256]{2,1,0:T(8,128)(2,1)S(1)} %collective-permute-done.9.refs_2_.refs_3_.refs_1_.refs_0_, bf16[4,64,256]{2,1,0:T(8,128)(2,1)S(1)} %pad_maximum_fusion.2.refs_1_, f32[8,56,256]{2,1,0:T(8,128)S(1)} %get-tuple-element.60.refs_3_.refs_2_, ...), custom_call_target="tpu_custom_call" | custom-call | flops 3200000000 | bytes 4000000 | tf_op jit(solution)/shard_map/pallas_call | solution.py:124
  73.7 1.0 %collective-permute-start.12 = (f32[8,8,256]{2,1,0:T(8,128)S(1)}, f32[8,8,256]{2,1,0:T(8,128)S(1)}, u32[]{:S(2)}, u32[]{:S(2)}) collective-permute-start(f32[8,8,256]{2,1,0:T(8,128)S(1)} %pad_maximum_fusion.3), channel_id=1, source_target_pairs={{0,2},{1,3},{2,0},{3,1},{4,6},{5,7},{6,4},{7,5},{8,10},{9,11},{10,... | collective-permute-start | bytes 196616 | tf_op jit(solution)/shard_map/ppermute | solution.py:146
  74.9 3.3 %shard_map.74 = (f32[4,56,256]{2,1,0:T(8,128)S(1)}, f32[4,8,256]{2,1,0:T(8,128)S(1)}) custom-call(bf16[8,64,256]{2,1,0:T(8,128)(2,1)S(1)} %collective-permute-done.9.refs_2_.refs_3_.refs_1_.refs_0_, bf16[4,64,256]{2,1,0:T(8,128)(2,1)S(1)} %pad_maximum_fusion.2.refs_1_, f32[4,56,256]{2,1,0:T(8,128)S(1)} %get-tuple-element.64.refs_2_, ...), custom_call_target="tpu_custom_call" | custom-call | flops 3200000000 | bytes 4000000 | tf_op jit(solution)/shard_map/pallas_call | solution.py:124
  78.2 1.8 %collective-permute-done.12 = f32[8,8,256]{2,1,0:T(8,128)S(1)} collective-permute-done((f32[8,8,256]{2,1,0:T(8,128)S(1)}, f32[8,8,256]{2,1,0:T(8,128)S(1)}, u32[]{:S(2)}, u32[]{:S(2)}) %collective-permute-start.12) | collective-permute-done | bytes 65568 | tf_op jit(solution)/shard_map/ppermute | solution.py:146
  80.0 1.8 %collective-permute-start.18 = (f32[4,8,256]{2,1,0:T(8,128)S(1)}, f32[4,8,256]{2,1,0:T(8,128)S(1)}, u32[]{:S(2)}, u32[]{:S(2)}) collective-permute-start(f32[4,8,256]{2,1,0:T(8,128)S(1)} %slice_add_fusion), channel_id=1, source_target_pairs={{0,34},{1,35},{2,32},{3,33},{4,38},{5,39},{6,36},{7,37},{8,42},{9,... | collective-permute-start | bytes 98312 | tf_op jit(solution)/shard_map/ppermute | solution.py:146
  81.9 3.1 %collective-permute-start.17 = (bf16[56,256]{1,0:T(8,128)(2,1)S(1)}, bf16[56,256]{1,0:T(8,128)(2,1)S(1)}, u32[]{:S(2)}, u32[]{:S(2)}) collective-permute-start(bf16[56,256]{1,0:T(8,128)(2,1)S(1)} %get-tuple-element.87), channel_id=1, source_target_pairs={{0,128},{1,129},{2,130},{3,131},{4,132},{5,133},{6,134},{7,135},{8... | collective-permute-start | bytes 86024 | tf_op jit(solution)/shard_map/ppermute | solution.py:146
  85.0 0.6 collective-permute-start.16
  85.6 1.1 %collective-permute-start.15 = (bf16[56,256]{1,0:T(8,128)(2,1)S(1)}, bf16[56,256]{1,0:T(8,128)(2,1)S(1)}, u32[]{:S(2)}, u32[]{:S(2)}) collective-permute-start(bf16[56,256]{1,0:T(8,128)(2,1)S(1)} %get-tuple-element.89), channel_id=1, source_target_pairs={{0,64},{1,65},{2,66},{3,67},{4,68},{5,69},{6,70},{7,71},{8,72},{9,... | collective-permute-start | bytes 86024 | tf_op jit(solution)/shard_map/ppermute | solution.py:146
  86.7 3.6 %collective-permute-start.21 = (f32[8,256]{1,0:T(8,128)S(1)}, f32[8,256]{1,0:T(8,128)S(1)}, u32[]{:S(2)}, u32[]{:S(2)}) collective-permute-start(f32[8,256]{1,0:T(8,128)S(1)} %get-tuple-element.90), channel_id=1, source_target_pairs={{0,8},{1,9},{2,10},{3,11},{4,12},{5,13},{6,14},{7,15},{8,0},{9,1},... | collective-permute-start | bytes 24584 | tf_op jit(solution)/shard_map/ppermute | solution.py:146
  90.3 1.2 %collective-permute-start.20 = (f32[8,256]{1,0:T(8,128)S(1)}, f32[8,256]{1,0:T(8,128)S(1)}, u32[]{:S(2)}, u32[]{:S(2)}) collective-permute-start(f32[8,256]{1,0:T(8,128)S(1)} %get-tuple-element.91), channel_id=1, source_target_pairs={{0,12},{1,13},{2,14},{3,15},{4,8},{5,9},{6,10},{7,11},{8,4},{9,5},... | collective-permute-start | bytes 24584 | tf_op jit(solution)/shard_map/ppermute | solution.py:146
  92.0 3.2 %collective-permute-done.20 = f32[8,256]{1,0:T(8,128)S(1)} collective-permute-done((f32[8,256]{1,0:T(8,128)S(1)}, f32[8,256]{1,0:T(8,128)S(1)}, u32[]{:S(2)}, u32[]{:S(2)}) %collective-permute-start.20) | collective-permute-done | bytes 8224 | tf_op jit(solution)/shard_map/ppermute | solution.py:146
  95.8 0.6 slice.60
  96.4 0.6 fusion
  (37 shorter events, 2.2 us)
Async XLA Ops:
  2.1 7.1 %collective-permute-start.2 = (bf16[1,64,256]{2,1,0:T(8,128)(2,1)}, bf16[1,64,256]{2,1,0:T(8,128)(2,1)S(1)}, u32[]{:S(2)}, u32[]{:S(2)}) collective-permute-start(bf16[1,64,256]{2,1,0:T(8,128)(2,1)} %get-tuple-element.44), channel_id=1, source_target_pairs={{0,8},{1,9},{2,10},{3,11},{4,12},{5,13},{6,14},{7,15},{8,0},{9,1},... | collective-permute-start | bytes 98312 | tf_op jit(solution)/shard_map/ppermute | solution.py:146
  5.1 5.9 %collective-permute-start.1 = (bf16[1,64,256]{2,1,0:T(8,128)(2,1)}, bf16[1,64,256]{2,1,0:T(8,128)(2,1)S(1)}, u32[]{:S(2)}, u32[]{:S(2)}) collective-permute-start(bf16[1,64,256]{2,1,0:T(8,128)(2,1)} %get-tuple-element.44), channel_id=1, source_target_pairs={{0,12},{1,13},{2,14},{3,15},{4,8},{5,9},{6,10},{7,11},{8,4},{9,5},... | collective-permute-start | bytes 98312 | tf_op jit(solution)/shard_map/ppermute | solution.py:146
  6.2 4.7 %collective-permute-start = (bf16[1,64,256]{2,1,0:T(8,128)(2,1)}, bf16[1,64,256]{2,1,0:T(8,128)(2,1)S(1)}, u32[]{:S(2)}, u32[]{:S(2)}) collective-permute-start(bf16[1,64,256]{2,1,0:T(8,128)(2,1)} %get-tuple-element.44), channel_id=1, source_target_pairs={{0,4},{1,5},{2,6},{3,7},{4,0},{5,1},{6,2},{7,3},{8,12},{9,13},{10,... | collective-permute-start | bytes 98312 | tf_op jit(solution)/shard_map/ppermute | solution.py:146
  6.2 7.1 %copy-start = (bf16[1,64,256]{2,1,0:T(8,128)(2,1)S(1)}, bf16[1,64,256]{2,1,0:T(8,128)(2,1)}, u32[]{:S(2)}) copy-start(bf16[1,64,256]{2,1,0:T(8,128)(2,1)} %get-tuple-element.45) | copy-start | bytes 98308
  6.2 5.7 %collective-permute-start.5 = (bf16[1,64,256]{2,1,0:T(8,128)(2,1)}, bf16[1,64,256]{2,1,0:T(8,128)(2,1)S(1)}, u32[]{:S(2)}, u32[]{:S(2)}) collective-permute-start(bf16[1,64,256]{2,1,0:T(8,128)(2,1)} %get-tuple-element.45), channel_id=1, source_target_pairs={{0,128},{1,129},{2,130},{3,131},{4,132},{5,133},{6,134},{7,135},{8... | collective-permute-start | bytes 98312 | tf_op jit(solution)/shard_map/ppermute | solution.py:146
  8.5 4.1 %collective-permute-start.4 = (bf16[1,64,256]{2,1,0:T(8,128)(2,1)}, bf16[1,64,256]{2,1,0:T(8,128)(2,1)S(1)}, u32[]{:S(2)}, u32[]{:S(2)}) collective-permute-start(bf16[1,64,256]{2,1,0:T(8,128)(2,1)} %get-tuple-element.45), channel_id=1, source_target_pairs={{0,192},{1,193},{2,194},{3,195},{4,196},{5,197},{6,198},{7,199},{8... | collective-permute-start | bytes 98312 | tf_op jit(solution)/shard_map/ppermute | solution.py:146
  9.2 4.1 %collective-permute-start.3 = (bf16[1,64,256]{2,1,0:T(8,128)(2,1)}, bf16[1,64,256]{2,1,0:T(8,128)(2,1)S(1)}, u32[]{:S(2)}, u32[]{:S(2)}) collective-permute-start(bf16[1,64,256]{2,1,0:T(8,128)(2,1)} %get-tuple-element.45), channel_id=1, source_target_pairs={{0,64},{1,65},{2,66},{3,67},{4,68},{5,69},{6,70},{7,71},{8,72},{9,... | collective-permute-start | bytes 98312 | tf_op jit(solution)/shard_map/ppermute | solution.py:146
  13.4 5.1 %collective-permute-start.8 = (bf16[4,64,256]{2,1,0:T(8,128)(2,1)S(1)}, bf16[4,64,256]{2,1,0:T(8,128)(2,1)S(1)}, u32[]{:S(2)}, u32[]{:S(2)}) collective-permute-start(bf16[4,64,256]{2,1,0:T(8,128)(2,1)S(1)} %pad_maximum_fusion.2.refs_1_), channel_id=1, source_target_pairs={{0,16},{1,17},{2,18},{3,19},{4,20},{5,21},{6,22},{7,23},{8,24},{9,... | collective-permute-start | bytes 393224 | tf_op jit(solution)/shard_map/ppermute | solution.py:146
  13.5 11.6 %collective-permute-start.6 = (bf16[4,64,256]{2,1,0:T(8,128)(2,1)S(1)}, bf16[4,64,256]{2,1,0:T(8,128)(2,1)S(1)}, u32[]{:S(2)}, u32[]{:S(2)}) collective-permute-start(bf16[4,64,256]{2,1,0:T(8,128)(2,1)S(1)} %pad_maximum_fusion.2.refs_1_), channel_id=1, source_target_pairs={{0,1},{1,0},{2,3},{3,2},{4,5},{5,4},{6,7},{7,6},{8,9},{9,8},{10,11... | collective-permute-start | bytes 393224 | tf_op jit(solution)/shard_map/ppermute | solution.py:146
  15.2 9.9 %collective-permute-start.7 = (bf16[4,64,256]{2,1,0:T(8,128)(2,1)S(1)}, bf16[4,64,256]{2,1,0:T(8,128)(2,1)S(1)}, u32[]{:S(2)}, u32[]{:S(2)}) collective-permute-start(bf16[4,64,256]{2,1,0:T(8,128)(2,1)S(1)} %pad_maximum_fusion.1.refs_0_), channel_id=1, source_target_pairs={{0,2},{1,3},{2,0},{3,1},{4,6},{5,7},{6,4},{7,5},{8,10},{9,11},{10,... | collective-permute-start | bytes 393224 | tf_op jit(solution)/shard_map/ppermute | solution.py:146
  25.1 13.4 %collective-permute-start.10 = (bf16[4,64,256]{2,1,0:T(8,128)(2,1)S(1)}, bf16[4,64,256]{2,1,0:T(8,128)(2,1)S(1)}, u32[]{:S(2)}, u32[]{:S(2)}) collective-permute-start(bf16[4,64,256]{2,1,0:T(8,128)(2,1)S(1)} %collective-permute-done.6.refs_3_), channel_id=1, source_target_pairs={{0,16},{1,17},{2,18},{3,19},{4,20},{5,21},{6,22},{7,23},{8,24},{9,... | collective-permute-start | bytes 393224 | tf_op jit(solution)/shard_map/ppermute | solution.py:146
  25.1 15.6 %collective-permute-start.9 = (bf16[8,64,256]{2,1,0:T(8,128)(2,1)S(1)}, bf16[8,64,256]{2,1,0:T(8,128)(2,1)S(1)}, u32[]{:S(2)}, u32[]{:S(2)}) collective-permute-start(bf16[8,64,256]{2,1,0:T(8,128)(2,1)S(1)} %pad_maximum_fusion), channel_id=1, source_target_pairs={{0,34},{1,35},{2,32},{3,33},{4,38},{5,39},{6,36},{7,37},{8,42},{9,... | collective-permute-start | bytes 786440 | tf_op jit(solution)/shard_map/ppermute | solution.py:146
  52.5 9.3 %collective-permute-start.11 = (f32[4,56,256]{2,1,0:T(8,128)S(1)}, f32[4,56,256]{2,1,0:T(8,128)S(1)}, u32[]{:S(2)}, u32[]{:S(2)}) collective-permute-start(f32[4,56,256]{2,1,0:T(8,128)S(1)} %get-tuple-element.58), channel_id=1, source_target_pairs={{0,16},{1,17},{2,18},{3,19},{4,20},{5,21},{6,22},{7,23},{8,24},{9,... | collective-permute-start | bytes 688136 | tf_op jit(solution)/shard_map/ppermute | solution.py:146
  61.8 18.2 %collective-permute-start.14 = (f32[4,56,256]{2,1,0:T(8,128)S(1)}, f32[4,56,256]{2,1,0:T(8,128)S(1)}, u32[]{:S(2)}, u32[]{:S(2)}) collective-permute-start(f32[4,56,256]{2,1,0:T(8,128)S(1)} %add.36), channel_id=1, source_target_pairs={{0,1},{1,0},{2,3},{3,2},{4,5},{5,4},{6,7},{7,6},{8,9},{9,8},{10,11... | collective-permute-start | bytes 688136 | tf_op jit(solution)/shard_map/ppermute | solution.py:146
  73.7 6.3 %collective-permute-start.12 = (f32[8,8,256]{2,1,0:T(8,128)S(1)}, f32[8,8,256]{2,1,0:T(8,128)S(1)}, u32[]{:S(2)}, u32[]{:S(2)}) collective-permute-start(f32[8,8,256]{2,1,0:T(8,128)S(1)} %pad_maximum_fusion.3), channel_id=1, source_target_pairs={{0,2},{1,3},{2,0},{3,1},{4,6},{5,7},{6,4},{7,5},{8,10},{9,11},{10,... | collective-permute-start | bytes 196616 | tf_op jit(solution)/shard_map/ppermute | solution.py:146
  74.7 5.3 %collective-permute-start.13 = (f32[4,56,256]{2,1,0:T(8,128)S(1)}, f32[4,56,256]{2,1,0:T(8,128)S(1)}, u32[]{:S(2)}, u32[]{:S(2)}) collective-permute-start(f32[4,56,256]{2,1,0:T(8,128)S(1)} %get-tuple-element.70), channel_id=1, source_target_pairs={{0,16},{1,17},{2,18},{3,19},{4,20},{5,21},{6,22},{7,23},{8,24},{9,... | collective-permute-start | bytes 688136 | tf_op jit(solution)/shard_map/ppermute | solution.py:146
  80.0 6.6 %collective-permute-start.18 = (f32[4,8,256]{2,1,0:T(8,128)S(1)}, f32[4,8,256]{2,1,0:T(8,128)S(1)}, u32[]{:S(2)}, u32[]{:S(2)}) collective-permute-start(f32[4,8,256]{2,1,0:T(8,128)S(1)} %slice_add_fusion), channel_id=1, source_target_pairs={{0,34},{1,35},{2,32},{3,33},{4,38},{5,39},{6,36},{7,37},{8,42},{9,... | collective-permute-start | bytes 98312 | tf_op jit(solution)/shard_map/ppermute | solution.py:146
  81.9 9.6 %collective-permute-start.17 = (bf16[56,256]{1,0:T(8,128)(2,1)S(1)}, bf16[56,256]{1,0:T(8,128)(2,1)S(1)}, u32[]{:S(2)}, u32[]{:S(2)}) collective-permute-start(bf16[56,256]{1,0:T(8,128)(2,1)S(1)} %get-tuple-element.87), channel_id=1, source_target_pairs={{0,128},{1,129},{2,130},{3,131},{4,132},{5,133},{6,134},{7,135},{8... | collective-permute-start | bytes 86024 | tf_op jit(solution)/shard_map/ppermute | solution.py:146
  85.0 6.5 %collective-permute-start.16 = (bf16[56,256]{1,0:T(8,128)(2,1)S(1)}, bf16[56,256]{1,0:T(8,128)(2,1)S(1)}, u32[]{:S(2)}, u32[]{:S(2)}) collective-permute-start(bf16[56,256]{1,0:T(8,128)(2,1)S(1)} %get-tuple-element.88), channel_id=1, source_target_pairs={{0,192},{1,193},{2,194},{3,195},{4,196},{5,197},{6,198},{7,199},{8... | collective-permute-start | bytes 86024 | tf_op jit(solution)/shard_map/ppermute | solution.py:146
  85.6 5.9 %collective-permute-start.15 = (bf16[56,256]{1,0:T(8,128)(2,1)S(1)}, bf16[56,256]{1,0:T(8,128)(2,1)S(1)}, u32[]{:S(2)}, u32[]{:S(2)}) collective-permute-start(bf16[56,256]{1,0:T(8,128)(2,1)S(1)} %get-tuple-element.89), channel_id=1, source_target_pairs={{0,64},{1,65},{2,66},{3,67},{4,68},{5,69},{6,70},{7,71},{8,72},{9,... | collective-permute-start | bytes 86024 | tf_op jit(solution)/shard_map/ppermute | solution.py:146
  86.7 5.3 %collective-permute-start.21 = (f32[8,256]{1,0:T(8,128)S(1)}, f32[8,256]{1,0:T(8,128)S(1)}, u32[]{:S(2)}, u32[]{:S(2)}) collective-permute-start(f32[8,256]{1,0:T(8,128)S(1)} %get-tuple-element.90), channel_id=1, source_target_pairs={{0,8},{1,9},{2,10},{3,11},{4,12},{5,13},{6,14},{7,15},{8,0},{9,1},... | collective-permute-start | bytes 24584 | tf_op jit(solution)/shard_map/ppermute | solution.py:146
  90.3 4.9 %collective-permute-start.20 = (f32[8,256]{1,0:T(8,128)S(1)}, f32[8,256]{1,0:T(8,128)S(1)}, u32[]{:S(2)}, u32[]{:S(2)}) collective-permute-start(f32[8,256]{1,0:T(8,128)S(1)} %get-tuple-element.91), channel_id=1, source_target_pairs={{0,12},{1,13},{2,14},{3,15},{4,8},{5,9},{6,10},{7,11},{8,4},{9,5},... | collective-permute-start | bytes 24584 | tf_op jit(solution)/shard_map/ppermute | solution.py:146
  91.5 3.7 %collective-permute-start.19 = (f32[8,256]{1,0:T(8,128)S(1)}, f32[8,256]{1,0:T(8,128)S(1)}, u32[]{:S(2)}, u32[]{:S(2)}) collective-permute-start(f32[8,256]{1,0:T(8,128)S(1)} %get-tuple-element.92), channel_id=1, source_target_pairs={{0,4},{1,5},{2,6},{3,7},{4,0},{5,1},{6,2},{7,3},{8,12},{9,13},{10,... | collective-permute-start | bytes 24584 | tf_op jit(solution)/shard_map/ppermute | solution.py:146
